TPU v7x, 32 devices: a whole 2x2x4 slice. The times are simulated.
32 devices in a mesh: rep: 4 (over x, core), fsdp: 8 (over z, y).
Axes of the slice: x: 2, y: 2, z: 4, core: 2. Of those that a mesh axis runs over, the one named last changes fastest.
Arguments:
- tokens: bfloat16 [32, 1024, 2048], P(('rep', 'fsdp')), may hold values from -6 to 6
- target: bfloat16 [32, 1024, 2048], P(('rep', 'fsdp')), may hold values from -6 to 6
- doc_lengths: int32 [32, 4], P(('rep', 'fsdp')), may hold values from 1 to 512, 1024 in all within a row
- corpus_ids: int32 [32, 1024], P(('rep', 'fsdp')), may hold values from 0 to 7
- corpus_weights: int32 [8], replicated, may hold values from 1 to 5
- w_in: float32 [2048, 3584], P('fsdp'), may hold values from -0.125 to 0.125
- w_out: float32 [2, 1024, 2048], P(None, 'fsdp'), may hold values from -0.375 to 0.375
- gains: float32 [2, 2048], P(None, 'fsdp'), may hold values from 0.5 to 1.5
- first_in: float32 [4, 2048, 3584], P('rep', 'fsdp'), may hold values from -40 to 40
- first_out: float32 [4, 2, 1024, 2048], P('rep', None, 'fsdp'), may hold values from -40 to 40
- first_gains: float32 [4, 2, 2048], P('rep', None, 'fsdp'), may hold values from -40 to 40
- second_in: float32 [4, 2048, 3584], P('rep', 'fsdp'), may hold values from 163.84 to 655.36
- second_out: float32 [4, 2, 1024, 2048], P('rep', None, 'fsdp'), may hold values from 163.84 to 655.36
- second_gains: float32 [4, 2, 2048], P('rep', None, 'fsdp'), may hold values from 163.84 to 655.36
- outer_in: float32 [2048, 3584], P('fsdp'), may hold values from -0.0625 to 0.0625
- outer_out: float32 [2, 1024, 2048], P(None, 'fsdp'), may hold values from -0.1875 to 0.1875
- outer_gains: float32 [2, 2048], P(None, 'fsdp'), may hold values from -3 to 3
Outputs:
- activations: bfloat16 [32, 1024, 2048], P(('rep', 'fsdp'))
- input_grad: bfloat16 [32, 1024, 2048], P(('rep', 'fsdp'))
- grad_in: float32 [4, 2048, 3584], P('rep', 'fsdp')
- grad_out: float32 [4, 2, 1024, 2048], P('rep', None, 'fsdp')
- grad_gains: float32 [4, 2, 2048], P('rep', None, 'fsdp')
- first_in_new: float32 [4, 2048, 3584], P('rep', 'fsdp')
- first_out_new: float32 [4, 2, 1024, 2048], P('rep', None, 'fsdp')
- first_gains_new: float32 [4, 2, 2048], P('rep', None, 'fsdp')
- second_in_new: float32 [4, 2048, 3584], P('rep', 'fsdp')
- second_out_new: float32 [4, 2, 1024, 2048], P('rep', None, 'fsdp')
- second_gains_new: float32 [4, 2, 2048], P('rep', None, 'fsdp')
- diff_in: float32 [2048, 3584], P('fsdp')
- diff_out: float32 [2, 1024, 2048], P(None, 'fsdp')
- diff_gains: float32 [2, 2048], P(None, 'fsdp')
- outer_in_new: float32 [2048, 3584], P('fsdp')
- outer_out_new: float32 [2, 1024, 2048], P(None, 'fsdp')
- outer_gains_new: float32 [2, 2048], P(None, 'fsdp')
- new_in: float32 [2048, 3584], P('fsdp')
- new_out: float32 [2, 1024, 2048], P(None, 'fsdp')
- new_gains: float32 [2, 2048], P(None, 'fsdp')
- copy_in: bfloat16 [2048, 3584], P('fsdp')
- copy_out: bfloat16 [2, 1024, 2048], P(None, 'fsdp')
- copy_gains: bfloat16 [2, 2048], P(None, 'fsdp')
Inputs may be any that keep to these rules, and one draw needn't show every extreme that they name: `doc_lengths`: each row's lengths sum to 1024.
All inputs are finite; a program needn't handle non-finite values.
Results may differ from a plain program's by a relative error of at most 0.023.
Values may be sent and summed in bfloat16 or wider, within the bound.
A program may use at most 448 MiB of HBM per device.

v0:
```python
import jax
import jax.numpy as jnp
from jax import lax
from jax.sharding import PartitionSpec as P

H = 16
HD = 64
KVH = 4
FF = 1024
LEN = 1024
NCORP = 8
STEP = 10


norm_eps = 1e-06
beta_first = 0.9
beta_second = 0.95
adam_eps = 1e-08
decay_rate = 0.1
rate_in = 0.02
rate_out = 0.08
rate_gains = 1.2
outer_decay = 0.5
outer_rate = 0.7
masked_score = -1e30


def doc_mask(lengths, offset, count):
    doc_ends = jnp.cumsum(lengths)
    position = jnp.arange(LEN, dtype=jnp.int32)
    doc_index = jnp.sum((position[:, None] >= doc_ends[None, :]).astype(jnp.int32), axis=1)
    row_docs = doc_index[offset : offset + count]
    row_place = position[offset : offset + count]
    return (row_docs[:, None] == doc_index[None, :]) & (row_place[:, None] >= position[None, :])


def adam_step(grad, first, second, weight, rate):
    first_new = beta_first * first + (1.0 - beta_first) * grad
    second_new = beta_second * second + (1.0 - beta_second) * grad * grad
    ratio = (
        first_new
        / (1.0 - beta_first**STEP)
        / (jnp.sqrt(second_new / (1.0 - beta_second**STEP)) + adam_eps)
    )
    local = weight - rate * (ratio + decay_rate * weight)
    return (first_new, second_new, weight - local)


def outer_step(delta_sum, momentum, weight, groups):
    average = delta_sum / groups
    momentum_new = outer_decay * momentum + average
    weight_new = weight - outer_rate * (average + outer_decay * momentum_new)
    return (average, momentum_new, weight_new)


def body(
    tokens,
    target,
    doc_lengths,
    corpus_ids,
    corpus_weights,
    w_in,
    w_out,
    gains,
    first_in,
    first_out,
    first_gains,
    second_in,
    second_out,
    second_gains,
    outer_in,
    outer_out,
    outer_gains,
):
    full_in, full_out, full_gains = (
        lax.all_gather(w_in.astype(jnp.bfloat16), "fsdp", axis=0, tiled=True),
        lax.all_gather(w_out.astype(jnp.bfloat16), "fsdp", axis=1, tiled=True),
        lax.all_gather(gains.astype(jnp.bfloat16), "fsdp", axis=1, tiled=True),
    )
    gain_pair = full_gains.astype(jnp.float32)
    group_size = H // KVH
    query_cols = H * HD
    key_cols = KVH * HD
    attn_cols = query_cols + 2 * key_cols
    block = min(512, LEN)
    score_scale = HD ** (-0.5)
    row_input = tokens[0].astype(jnp.float32)
    lengths = doc_lengths[0]
    inverse_one = lax.rsqrt(jnp.mean(row_input * row_input, axis=-1, keepdims=True) + norm_eps)
    normed_one = row_input * inverse_one
    first_low = (normed_one * gain_pair[0]).astype(jnp.bfloat16)
    packed = jnp.dot(first_low, full_in[:, :attn_cols], preferred_element_type=jnp.float32).astype(
        jnp.bfloat16
    )
    queries = packed[:, :query_cols].reshape(LEN, KVH, group_size, HD)
    key_heads = packed[:, query_cols : query_cols + key_cols].reshape(LEN, KVH, HD)
    value_heads = packed[:, query_cols + key_cols :].reshape(LEN, KVH, HD)
    mixed_blocks = []
    log_totals = []
    for offset in range(0, LEN, block):
        allowed = doc_mask(lengths, offset, block)
        scores = (
            jnp.einsum(
                "qkgd,skd->kgqs",
                queries[offset : offset + block],
                key_heads,
                preferred_element_type=jnp.float32,
            )
            * score_scale
        )
        scores = jnp.where(allowed, scores, masked_score)
        row_max = jnp.max(scores, axis=-1, keepdims=True)
        exp_terms = jnp.exp(scores - row_max)
        row_total = jnp.sum(exp_terms, axis=-1, keepdims=True)
        probs_low = (exp_terms / row_total).astype(jnp.bfloat16)
        block_out = jnp.einsum(
            "kgqs,skd->qkgd", probs_low, value_heads, preferred_element_type=jnp.float32
        )
        mixed_blocks.append(block_out.reshape(block, query_cols))
        log_totals.append(row_max + jnp.log(row_total))
    mixed_low = jnp.concatenate(mixed_blocks, axis=0).astype(jnp.bfloat16)
    middle = row_input + jnp.dot(mixed_low, full_out[0], preferred_element_type=jnp.float32)
    inverse_two = lax.rsqrt(jnp.mean(middle * middle, axis=-1, keepdims=True) + norm_eps)
    normed_two = middle * inverse_two
    second_low = (normed_two * gain_pair[1]).astype(jnp.bfloat16)
    both = jnp.dot(second_low, full_in[:, attn_cols:], preferred_element_type=jnp.float32)
    gate = both[:, :FF]
    upward = both[:, FF:]
    sigmoid_gate = jax.nn.sigmoid(gate)
    silu_gate = gate * sigmoid_gate
    hidden_low = (silu_gate * upward).astype(jnp.bfloat16)
    activations = (
        middle + jnp.dot(hidden_low, full_out[1], preferred_element_type=jnp.float32)
    ).astype(jnp.bfloat16)
    back_in, back_out, back_gains = (
        lax.all_gather(w_in.astype(jnp.bfloat16), "fsdp", axis=0, tiled=True),
        lax.all_gather(w_out.astype(jnp.bfloat16), "fsdp", axis=1, tiled=True),
        lax.all_gather(gains.astype(jnp.bfloat16), "fsdp", axis=1, tiled=True),
    )
    back_pair = back_gains.astype(jnp.float32)
    corpus_range = jnp.arange(NCORP, dtype=jnp.int32)
    table = corpus_weights.astype(jnp.float32) / 4.0
    token_weight = jnp.sum(
        jnp.where(corpus_ids[0][:, None] == corpus_range[None, :], table[None, :], 0.0), axis=1
    )
    out_grad = token_weight[:, None] * target[0].astype(jnp.float32)
    out_low = out_grad.astype(jnp.bfloat16)
    grad_down = jnp.einsum("tf,td->fd", hidden_low, out_low, preferred_element_type=jnp.float32)
    d_hidden = jnp.einsum("td,fd->tf", out_low, back_out[1], preferred_element_type=jnp.float32)
    d_gate = d_hidden * upward * sigmoid_gate * (1.0 + gate * (1.0 - sigmoid_gate))
    d_upward = d_hidden * silu_gate
    d_both = jnp.concatenate([d_gate, d_upward], axis=1).astype(jnp.bfloat16)
    d_second = jnp.einsum(
        "tf,cf->tc", d_both, back_in[:, attn_cols:], preferred_element_type=jnp.float32
    )
    gain_two = jnp.sum(d_second * normed_two, axis=0)
    scaled_two = d_second * back_pair[1]
    d_middle = out_grad + inverse_two * (
        scaled_two - normed_two * jnp.mean(scaled_two * normed_two, axis=-1, keepdims=True)
    )
    middle_low = d_middle.astype(jnp.bfloat16)
    grad_proj = jnp.einsum("tc,td->cd", mixed_low, middle_low, preferred_element_type=jnp.float32)
    d_mixed = jnp.einsum(
        "td,cd->tc", middle_low, back_out[0], preferred_element_type=jnp.float32
    ).astype(jnp.bfloat16)
    grad_out_full = jnp.stack([grad_proj, grad_down])
    d_mixed_heads = d_mixed.reshape(LEN, KVH, group_size, HD)
    d_key_heads = jnp.zeros((LEN, KVH, HD), jnp.float32)
    d_value_heads = jnp.zeros((LEN, KVH, HD), jnp.float32)
    d_query_blocks = []
    for block_index, offset in enumerate(range(0, LEN, block)):
        allowed = doc_mask(lengths, offset, block)
        block_queries = queries[offset : offset + block]
        scores = (
            jnp.einsum(
                "qkgd,skd->kgqs", block_queries, key_heads, preferred_element_type=jnp.float32
            )
            * score_scale
        )
        scores = jnp.where(allowed, scores, masked_score)
        attn_probs = jnp.exp(scores - log_totals[block_index])
        probs_low = attn_probs.astype(jnp.bfloat16)
        block_grad = d_mixed_heads[offset : offset + block]
        d_value_heads = d_value_heads + jnp.einsum(
            "kgqs,qkgd->skd", probs_low, block_grad, preferred_element_type=jnp.float32
        )
        d_probs = jnp.einsum(
            "qkgd,skd->kgqs", block_grad, value_heads, preferred_element_type=jnp.float32
        )
        inner = jnp.sum(attn_probs * d_probs, axis=-1, keepdims=True)
        d_scores = (attn_probs * (d_probs - inner)).astype(jnp.bfloat16)
        d_query_blocks.append(
            jnp.einsum("kgqs,skd->qkgd", d_scores, key_heads, preferred_element_type=jnp.float32)
            * score_scale
        )
        d_key_heads = (
            d_key_heads
            + jnp.einsum(
                "kgqs,qkgd->skd", d_scores, block_queries, preferred_element_type=jnp.float32
            )
            * score_scale
        )
    d_queries = jnp.concatenate(d_query_blocks, axis=0).reshape(LEN, query_cols)
    d_packed = jnp.concatenate(
        [d_queries, d_key_heads.reshape(LEN, key_cols), d_value_heads.reshape(LEN, key_cols)],
        axis=1,
    ).astype(jnp.bfloat16)
    d_first = jnp.einsum(
        "tf,cf->tc", d_packed, back_in[:, :attn_cols], preferred_element_type=jnp.float32
    )
    gain_one = jnp.sum(d_first * normed_one, axis=0)
    scaled_one = d_first * back_pair[0]
    input_grad = (
        d_middle
        + inverse_one
        * (scaled_one - normed_one * jnp.mean(scaled_one * normed_one, axis=-1, keepdims=True))
    ).astype(jnp.bfloat16)
    gain_full = jnp.stack([gain_one, gain_two])
    grad_attn = jnp.einsum("tc,tf->cf", first_low, d_packed, preferred_element_type=jnp.float32)
    grad_ffn = jnp.einsum("tc,tf->cf", second_low, d_both, preferred_element_type=jnp.float32)
    grad_in_full = jnp.concatenate([grad_attn, grad_ffn], axis=1)
    grad_in_share, grad_out_share, gain_share = (
        lax.psum_scatter(
            grad_in_full.astype(jnp.bfloat16), "fsdp", scatter_dimension=0, tiled=True
        ).astype(jnp.float32),
        lax.psum_scatter(
            grad_out_full.astype(jnp.bfloat16), "fsdp", scatter_dimension=1, tiled=True
        ).astype(jnp.float32),
        lax.psum_scatter(
            gain_full.astype(jnp.bfloat16), "fsdp", scatter_dimension=1, tiled=True
        ).astype(jnp.float32),
    )
    first_in_new, second_in_new, delta_in = adam_step(
        grad_in_share, first_in[0], second_in[0], w_in, rate_in
    )
    first_out_new, second_out_new, delta_out = adam_step(
        grad_out_share, first_out[0], second_out[0], w_out, rate_out
    )
    first_gains_new, second_gains_new, delta_gains = adam_step(
        gain_share, first_gains[0], second_gains[0], gains, rate_gains
    )
    sum_in, sum_out, sum_gains = (
        lax.psum(delta_in.astype(jnp.bfloat16), "rep").astype(jnp.float32),
        lax.psum(delta_out.astype(jnp.bfloat16), "rep").astype(jnp.float32),
        lax.psum(delta_gains.astype(jnp.bfloat16), "rep").astype(jnp.float32),
    )
    groups = lax.axis_size("rep")
    diff_in, outer_in_new, new_in = outer_step(sum_in, outer_in, w_in, groups)
    diff_out, outer_out_new, new_out = outer_step(sum_out, outer_out, w_out, groups)
    diff_gains, outer_gains_new, new_gains = outer_step(sum_gains, outer_gains, gains, groups)
    return (
        activations[None],
        input_grad[None],
        grad_in_share[None],
        grad_out_share[None],
        gain_share[None],
        first_in_new[None],
        first_out_new[None],
        first_gains_new[None],
        second_in_new[None],
        second_out_new[None],
        second_gains_new[None],
        diff_in,
        diff_out,
        diff_gains,
        outer_in_new,
        outer_out_new,
        outer_gains_new,
        new_in,
        new_out,
        new_gains,
        new_in.astype(jnp.bfloat16),
        new_out.astype(jnp.bfloat16),
        new_gains.astype(jnp.bfloat16),
    )


def solution(mesh):
    placed = (
        P(("rep", "fsdp"), None, None),
        P(("rep", "fsdp"), None, None),
        P(("rep", "fsdp"), None),
        P(("rep", "fsdp"), None),
        P(),
        P("fsdp", None),
        P(None, "fsdp", None),
        P(None, "fsdp"),
        P("rep", "fsdp", None),
        P("rep", None, "fsdp", None),
        P("rep", None, "fsdp"),
        P("rep", "fsdp", None),
        P("rep", None, "fsdp", None),
        P("rep", None, "fsdp"),
        P("fsdp", None),
        P(None, "fsdp", None),
        P(None, "fsdp"),
    )
    return jax.shard_map(
        body,
        mesh=mesh,
        in_specs=placed,
        out_specs=(
            P(("rep", "fsdp"), None, None),
            P(("rep", "fsdp"), None, None),
            P("rep", "fsdp", None),
            P("rep", None, "fsdp", None),
            P("rep", None, "fsdp"),
            P("rep", "fsdp", None),
            P("rep", None, "fsdp", None),
            P("rep", None, "fsdp"),
            P("rep", "fsdp", None),
            P("rep", None, "fsdp", None),
            P("rep", None, "fsdp"),
            P("fsdp", None),
            P(None, "fsdp", None),
            P(None, "fsdp"),
            P("fsdp", None),
            P(None, "fsdp", None),
            P(None, "fsdp"),
            P("fsdp", None),
            P(None, "fsdp", None),
            P(None, "fsdp"),
            P("fsdp", None),
            P(None, "fsdp", None),
            P(None, "fsdp"),
        ),
        check_vma=False,
    )
```

profile of v0, /device:TPU:0, one launch (start us, length us, event | category | flops | bytes accessed | tf_op | source)
XLA Modules:
  0.0 1196.0 jit_solution(10268942916999943711)
XLA Ops:
  7.3 3.6 convert_element_type.137
  12.2 22.4 %all_gather.12 = bf16[2,2048]{1,0:T(2,128)(2,1)S(1)} all-gather(bf16[2,256]{1,0:T(2,128)(2,1)S(1)} %convert_element_type.134), channel_id=1, replica_groups=mesh['rep'=4,'fsdp'=8] {'fsdp'}, dimensions={1}, use_global_device_ids=true | all-gather | bytes 9216 | tf_op jit(solution)/shard_map/all_gather | solution.py:78
  35.2 3.1 fusion.35
  40.2 175.5 %all-gather.3.cloned.1.call-done = bf16[2048,3584]{1,0:T(8,128)(2,1)} async-done(((bf16[256,3584]{1,0:T(8,128)(2,1)}), bf16[2048,3584]{1,0:T(8,128)(2,1)}) %all-gather.3.cloned.1.call-update) | async-done | bytes 14680080 | tf_op jit(solution)/shard_map/all_gather | solution.py:76
  215.7 10.3 fusion.56
  226.9 1.3 fusion.120
  228.4 1.2 copy.133
  229.7 1.3 copy.136
  231.0 1.5 copy.134
  232.5 15.2 %fusion.23 = (f32[4,4,512]{2,1,0:T(4,128)S(1)}, f32[4,1024,512,4]{2,1,3,0:T(8,128)}) fusion(pred[512,1024]{0,1:T(8,128)(4,1)S(1)} %get-tuple-element.151, bf16[1024,4,64,1]{0,2,3,1:T(8,128)(2,1)S(1)} %bitcast.252, bf16[512,4,4,64]{0,3,2,1:T(8,128)(2,1)} %bitcast.258), kind=kOutput, calls=%fused_computation.37 | convolution fusion | flops 1098899456 | bytes 35684352 | tf_op jit(solution)/shard_map/qkgd,skd->kgqs/dot_general | solution.py:103
  247.7 13.4 %fusion.22 = (f32[4,4,512]{2,1,0:T(4,128)S(1)}, f32[4,1024,512,4]{2,1,3,0:T(8,128)}) fusion(pred[512,1024]{0,1:T(8,128)(4,1)S(1)} %get-tuple-element.150, bf16[1024,4,64,1]{0,2,3,1:T(8,128)(2,1)S(1)} %bitcast.253, bf16[512,4,4,64]{0,3,2,1:T(8,128)(2,1)S(1)} %bitcast.256), kind=kOutput, calls=%fused_computation.36 | convolution fusion | flops 1098899456 | bytes 35684352 | tf_op jit(solution)/shard_map/qkgd,skd->kgqs/dot_general | solution.py:103
  261.1 16.0 %fusion.7 = f32[4,4,512]{2,1,0:T(4,128)S(1)} fusion(f32[4,4,512]{2,1,0:T(4,128)S(1)} %get-tuple-element.157, f32[4,1024,512,4]{2,1,3,0:T(8,128)} %get-tuple-element.158, pred[512,1024]{0,1:T(8,128)(4,1)S(1)} %get-tuple-element.151), kind=kLoop, calls=%fused_computation.19 | loop fusion | flops 33546240 | bytes 34144256 | tf_op jit(solution)/shard_map/reduce_sum | solution.py:114
  277.1 5.5 copy-done
  282.5 7.0 fusion.6
  289.6 14.7 %fusion.75 = bf16[4,64,4,512]{3,1,2,0:T(8,128)(2,1)S(1)} fusion(bf16[1024,4,64,1]{0,2,3,1:T(8,128)(2,1)S(1)} %bitcast.260, f32[4,4,512]{2,1,0:T(4,128)S(1)} %fusion.7, f32[4,4,512]{2,1,0:T(4,128)S(1)} %get-tuple-element.157, f32[4,1024,512,4]{2,1,3,0:T(8,128)} %get-tuple-element.158, pred[512,1024]{0,1:T(8,128)(4,1)S(1)} %get-tuple-element.151), kind=kOutput, calls=%fused_computation.123 | convolution fusion | flops 1116209152 | bytes 35717120 | tf_op jit(solution)/shard_map/kgqs,skd->qkgd/dot_general | solution.py:116
  304.3 15.8 %fusion.76 = bf16[4,64,4,512]{3,1,2,0:T(8,128)(2,1)} fusion(bf16[1024,4,64,1]{0,2,3,1:T(8,128)(2,1)S(1)} %bitcast.261, f32[4,4,512]{2,1,0:T(4,128)S(1)} %fusion.6, f32[4,4,512]{2,1,0:T(4,128)S(1)} %get-tuple-element.159, f32[4,1024,512,4]{2,1,3,0:T(8,128)} %get-tuple-element.160, pred[512,1024]{0,1:T(8,128)(4,1)S(1)} %get-tuple-element.150), kind=kOutput, calls=%fused_computation.124 | convolution fusion | flops 1116209152 | bytes 35717120 | tf_op jit(solution)/shard_map/kgqs,skd->qkgd/dot_general | solution.py:116
  320.1 21.5 %all-gather.5.cloned.1.call-done = bf16[2,1024,2048]{2,1,0:T(8,128)(2,1)} async-done(((bf16[2,128,2048]{2,1,0:T(8,128)(2,1)}), bf16[2,1024,2048]{2,1,0:T(8,128)(2,1)}) %all-gather.5.cloned.1.call-update) | async-done | bytes 8388624 | tf_op jit(solution)/shard_map/all_gather | solution.py:77
  341.6 9.2 multiply_reduce_fusion.2
  350.9 3.3 copy-done.13
  354.2 14.2 %fusion.38 = f32[1024,2048]{1,0:T(8,128)} fusion(bf16[2048,3584]{1,0:T(8,128)(2,1)} %all-gather.3.cloned.1.call-done, f32[1024,2048]{1,0:T(8,128)S(1)} %get-tuple-element.162, f32[2048]{0:T(1024)S(1)} %bitcast.288, f32[1024]{0:T(1024)S(1)} %add_rsqrt_fusion), kind=kOutput, calls=%fused_computation.62 | convolution fusion | flops 8596226048 | bytes 25178112 | tf_op jit(solution)/shard_map/dot_general | solution.py:126
  368.3 11.2 multiply_convert_fusion.2
  379.5 18.0 %multiply_reduce_fusion = (bf16[2048]{0:T(1024)(128)(2,1)}, f32[1024]{0:T(1024)S(1)}, f32[1024,2048]{1,0:T(8,128)}) fusion(f32[1024,2048]{1,0:T(8,128)} %copy-done.13, f32[1024]{0:T(1024)S(1)} %add_rsqrt_fusion, f32[2048]{0:T(1024)S(1)} %bitcast.289, bf16[2048,3584]{1,0:T(8,128)(2,1)} %all-gather.3.cloned.1.call-done, ...), kind=kOutput, calls=%fused_computation.53 | convolution fusion | flops 8610903040 | bytes 29380608 | tf_op jit(solution)/shard_map/tf,cf->tc/dot_general | solution.py:153
  397.5 8.8 fusion.26
  406.3 10.0 fusion.71
  416.3 1.1 fusion.122
  417.4 16.0 %fusion.77 = f32[4,64,1024]{2,1,0:T(8,128)} fusion(bf16[512,4,4,64]{0,3,2,1:T(8,128)(2,1)} %bitcast.266, f32[4,4,512]{2,1,0:T(4,128)S(1)} %bitcast.276, f32[4,1024,512,4]{2,1,3,0:T(8,128)} %get-tuple-element.160, pred[512,1024]{0,1:T(8,128)(4,1)S(1)} %get-tuple-element.150), kind=kOutput, calls=%fused_computation.125 | convolution fusion | flops 1107296256 | bytes 36208640 | tf_op jit(solution)/shard_map/kgqs,qkgd->skd/dot_general | solution.py:184
  433.4 24.0 %fusion.3 = (f32[4,4,512]{2,1,0:T(4,128)S(1)}, f32[4,1024,512,4]{2,1,3,0:T(8,128)}) fusion(f32[4,4,512]{2,1,0:T(4,128)S(1)} %bitcast.277, f32[4,1024,512,4]{2,1,3,0:T(8,128)} %get-tuple-element.160, pred[512,1024]{0,1:T(8,128)(4,1)S(1)} %get-tuple-element.150, bf16[1024,4,64,1]{0,2,3,1:T(8,128)(2,1)S(1)} %bitcast.262, bf16[512,4,4,64]{0,3,2,1:T(8,128)(2,1)} %bitcast.267), kind=kOutput, calls=%fused_computation.7 | convolution fusion | flops 1115676672 | bytes 69271552 | tf_op jit(solution)/shard_map/qkgd,skd->kgqs/dot_general | solution.py:187
  457.4 23.7 %fusion = (f32[4,4,512]{2,1,0:T(4,128)S(1)}, f32[4,1024,512,4]{2,1,3,0:T(8,128)}) fusion(f32[4,4,512]{2,1,0:T(4,128)S(1)} %bitcast.273, f32[4,1024,512,4]{2,1,3,0:T(8,128)} %get-tuple-element.158, pred[512,1024]{0,1:T(8,128)(4,1)S(1)} %copy-done.2, bf16[1024,4,64,1]{0,2,3,1:T(8,128)(2,1)S(1)} %bitcast.263, bf16[512,4,4,64]{0,3,2,1:T(8,128)(2,1)S(1)} %bitcast.264), kind=kOutput, calls=%fused_computation.2 | convolution fusion | flops 1115676672 | bytes 69271552 | tf_op jit(solution)/shard_map/qkgd,skd->kgqs/dot_general | solution.py:187
  481.1 55.6 %fusion.2 = (bf16[4,4,512,1024]{2,3,1,0:T(8,128)(2,1)}, bf16[4,4,512,1024]{2,3,1,0:T(8,128)(2,1)}) fusion(f32[4,1024,512,4]{2,1,3,0:T(8,128)} %get-tuple-element.165, f32[4,4,512]{2,1,0:T(4,128)S(1)} %get-tuple-element.164, f32[4,4,512]{2,1,0:T(4,128)S(1)} %bitcast.274, f32[4,1024,512,4]{2,1,3,0:T(8,128)} %get-tuple-element.158, ...), kind=kLoop, calls=%fused_computation.4 | loop fusion | flops 100663296 | bytes 168951808 | tf_op jit(solution)/shard_map/convert_element_type | solution.py:191
  536.8 10.9 convolution_bitcast_fusion
  547.8 9.9 fusion.84
  557.7 9.5 convert_bitcast_fusion.3
  567.1 16.2 %fusion.91 = bf16[4,64,1024]{2,1,0:T(8,128)(2,1)} fusion(f32[4,64,1024]{2,1,0:T(8,128)} %fusion.77, bf16[512,4,4,64]{0,3,2,1:T(8,128)(2,1)S(1)} %bitcast.265, f32[4,4,512]{2,1,0:T(4,128)S(1)} %bitcast.275, f32[4,1024,512,4]{2,1,3,0:T(8,128)} %get-tuple-element.158, pred[512,1024]{0,1:T(8,128)(4,1)S(1)} %copy-done.2), kind=kOutput, calls=%fused_computation.135 | convolution fusion | flops 1107820544 | bytes 36732928 | tf_op jit(solution)/shard_map/kgqs,qkgd->skd/dot_general | solution.py:184
  583.4 9.8 fusion.83
  593.2 10.9 fusion.90
  604.2 9.8 convert_bitcast_fusion.2
  614.4 15.6 %fusion.34 = (bf16[2048]{0:T(1024)(128)(2,1)S(1)}, f32[1024]{0:T(1024)S(1)}, f32[1024,2048]{1,0:T(8,128)}) fusion(bf16[1,1024,2048]{2,1,0:T(8,128)(2,1)S(1)} %copy-done.6, f32[1024]{0:T(1024)S(1)} %copy-done.39, f32[2048]{0:T(1024)S(1)} %bitcast.285, bf16[2048,3584]{1,0:T(8,128)(2,1)} %all-gather.3.cloned.1.call-done, bf16[1024,256]{0,1:T(8,128)(2,1)S(1)} %bitcast.299, ...), kind=kOutput, calls=%fused_computation.50 | convolution fusion | flops 6466565120 | bytes 22040576 | tf_op jit(solution)/shard_map/tf,cf->tc/dot_general | solution.py:208
  631.2 7.5 pad_maximum_fusion.1
  639.4 13.3 %convolution_convert_fusion.1 = bf16[2048,2048]{0,1:T(8,128)(2,1)S(1)} fusion(bf16[1024,1024]{1,0:T(8,128)(2,1)} %get-tuple-element.132, bf16[1024,1024]{1,0:T(8,128)(2,1)} %copy-done.52, f32[1024,2048]{1,0:T(8,128)} %copy-done.13, f32[2048]{0:T(1024)S(1)} %bitcast.291, f32[1024]{0:T(1024)S(1)} %copy-done.37), kind=kOutput, calls=%fused_computation.59 | convolution fusion | flops 8608808960 | bytes 20983808 | tf_op jit(solution)/shard_map/tc,tf->cf/dot_general | solution.py:220
  652.8 8.8 convolution_convert_fusion
  661.6 16.6 %pad_maximum_fusion = bf16[2048,3584]{0,1:T(8,128)(2,1)} fusion(bf16[2048,2048]{0,1:T(8,128)(2,1)S(1)} %convolution_convert_fusion.1, bf16[2048,1536]{0,1:T(8,128)(2,1)S(1)} %convolution_convert_fusion), kind=kLoop, calls=%fused_computation.28 | loop fusion | flops 29360128 | bytes 29360128 | tf_op jit(solution)/shard_map/concatenate | solution.py:221
  678.2 5.4 copy.150
  683.6 5.1 copy.146
  688.7 5.1 copy.147
  693.9 5.1 copy.151
  699.0 11.1 fusion.45
  710.2 9.7 fusion.44
  721.5 6.5 psum.23
  729.2 114.2 %reduce-scatter.8.cloned.1.call-done = bf16[2,128,2048]{2,1,0:T(8,128)(2,1)} async-done(((bf16[2,1024,2048]{2,1,0:T(8,128)(2,1)}), bf16[2,128,2048]{2,1,0:T(8,128)(2,1)}) %reduce-scatter.8.cloned.1.call-update) | async-done | bytes 1048592 | tf_op jit(solution)/shard_map/reduce_scatter | solution.py:226
  843.4 6.3 fusion.64
  849.7 233.1 %reduce-scatter.6.cloned.1.call-done = bf16[256,3584]{0,1:T(8,128)(2,1)} async-done(((bf16[2048,3584]{0,1:T(8,128)(2,1)}), bf16[256,3584]{0,1:T(8,128)(2,1)}) %reduce-scatter.6.cloned.1.call-update) | async-done | bytes 1835024 | tf_op jit(solution)/shard_map/reduce_scatter | solution.py:223
  1082.8 8.7 fusion.60
  1091.5 1.6 convert_bitcast_fusion.4
  1093.1 3.6 convert_bitcast_fusion.1
  1096.7 5.1 copy.153
  1101.8 5.1 copy.154
  1107.0 5.2 copy.155
  1112.1 43.0 %all-reduce.3.cloned.1.call-done = (bf16[256,3584]{0,1:T(8,128)(2,1)}, bf16[2,128,2048]{2,1,0:T(8,128)(2,1)}) async-done(((bf16[256,3584]{0,1:T(8,128)(2,1)}, bf16[2,128,2048]{2,1,0:T(8,128)(2,1)}), (bf16[256,3584]{0,1:T(8,128)(2,1)}, bf16[2,128,2048]{2,1,0:T(8,128)(2,1)})) %all-reduce.3.cloned.1.call-update) | async-done | bytes 2883600 | tf_op jit(solution)/shard_map/psum | solution.py:243
  1155.1 9.2 fusion.119
  1164.3 5.1 copy.156
  1169.5 5.1 copy.157
  1174.6 5.2 copy.158
  1179.8 3.8 copy.159
  1183.6 5.3 fusion.118
  (147 shorter events, 9.9 us)
Async XLA Ops:
  7.2 3.7 copy-start.4
  7.2 4.9 copy-start.32
  7.2 208.5 %all-gather.3.cloned.1.call-start = ((), (), s32[]{:S(2)}) async-start(), calls=%async_computation.3 | async-start | bytes 16515072 | tf_op jit(solution)/shard_map/all_gather | solution.py:76
  10.8 27.5 %copy-start.45 = (s32[1,4]{1,0:T(1,128)S(1)}, s32[1,4]{1,0:T(1,128)}, u32[]{:S(2)}) copy-start(s32[1,4]{1,0:T(1,128)} %param.19) | copy-start | bytes 52
  10.9 27.8 %copy-start.46 = (s32[8]{0:T(128)S(1)}, s32[8]{0:T(128)}, u32[]{:S(2)}) copy-start(s32[8]{0:T(128)} %param.21) | copy-start | bytes 100
  10.9 27.8 %copy-start.41 = (s32[1,1024]{1,0:T(1,128)S(1)}, s32[1,1024]{1,0:T(1,128)}, u32[]{:S(2)}) copy-start(s32[1,1024]{1,0:T(1,128)} %param.20) | copy-start | bytes 12292
  10.9 330.7 %all-gather.5.cloned.1.call-start = ((), (), s32[]{:S(2)}) async-start(), calls=%async_computation.4 | async-start | bytes 9437184 | tf_op jit(solution)/shard_map/all_gather | solution.py:77
  12.1 707.8 %reduce-scatter.10.cloned.1.call-start = ((), (), s32[]{:S(2)}) async-start(), calls=%async_computation.7 | async-start | bytes 589824
  35.2 180.5 %copy-start.28 = (f32[1,2048]{1,0:T(1,128)}, f32[1,2048]{1,0:T(1,128)S(1)}, u32[]{:S(2)}) copy-start(f32[1,2048]{1,0:T(1,128)S(1)} %get-tuple-element.149) | copy-start | bytes 24580
  38.3 177.4 %copy-start.38 = (f32[1024]{0:T(1024)}, f32[1024]{0:T(1024)S(1)}, u32[]{:S(2)}) copy-start(f32[1024]{0:T(1024)S(1)} %add_rsqrt_fusion.1) | copy-start | bytes 12292
  40.2 249.3 %copy-start.1 = (pred[512,1024]{0,1:T(8,128)(4,1)}, pred[512,1024]{0,1:T(8,128)(4,1)S(1)}, u32[]{:S(2)}) copy-start(pred[512,1024]{0,1:T(8,128)(4,1)S(1)} %get-tuple-element.151) | copy-start | bytes 1572868
  229.6 18.0 %copy-start.8 = (bf16[1024,256]{0,1:T(8,128)(2,1)}, bf16[1024,256]{0,1:T(8,128)(2,1)S(1)}, u32[]{:S(2)}) copy-start(bf16[1024,256]{0,1:T(8,128)(2,1)S(1)} %copy.133) | copy-start | bytes 1572868
  232.5 15.2 %copy-start.10 = (bf16[512,1024]{0,1:T(8,128)(2,1)}, bf16[512,1024]{0,1:T(8,128)(2,1)S(1)}, u32[]{:S(2)}) copy-start(bf16[512,1024]{0,1:T(8,128)(2,1)S(1)} %copy.134) | copy-start | bytes 3145732
  247.7 41.9 %copy-start.24 = (f32[4,4,512]{2,1,0:T(4,128)}, f32[4,4,512]{2,1,0:T(4,128)S(1)}, u32[]{:S(2)}) copy-start(f32[4,4,512]{2,1,0:T(4,128)S(1)} %get-tuple-element.157) | copy-start | bytes 98308
  261.1 21.5 %copy-start = (f32[4,1024,512,4]{2,1,3,0:T(8,128)S(1)}, f32[4,1024,512,4]{2,1,3,0:T(8,128)}, u32[]{:S(2)}) copy-start(f32[4,1024,512,4]{2,1,3,0:T(8,128)} %get-tuple-element.160) | copy-start | bytes 100663296
  277.1 12.5 %copy-start.26 = (f32[4,4,512]{2,1,0:T(4,128)}, f32[4,4,512]{2,1,0:T(4,128)S(1)}, u32[]{:S(2)}) copy-start(f32[4,4,512]{2,1,0:T(4,128)S(1)} %fusion.7) | copy-start | bytes 98308
  304.3 37.3 %copy-start.47 = (bf16[4,64,4,512]{3,1,2,0:T(8,128)(2,1)}, bf16[4,64,4,512]{3,1,2,0:T(8,128)(2,1)S(1)}, u32[]{:S(2)}) copy-start(bf16[4,64,4,512]{3,1,2,0:T(8,128)(2,1)S(1)} %fusion.75) | copy-start | bytes 3145732
  341.6 12.5 %copy-start.30 = (f32[1,2048]{1,0:T(1,128)S(1)}, f32[1,2048]{1,0:T(1,128)}, u32[]{:S(2)}) copy-start(f32[1,2048]{1,0:T(1,128)} %get-tuple-element.148) | copy-start | bytes 24580
  350.8 3.3 copy-start.13
  350.9 46.7 %copy-start.36 = (f32[1024]{0:T(1024)}, f32[1024]{0:T(1024)S(1)}, u32[]{:S(2)}) copy-start(f32[1024]{0:T(1024)S(1)} %add_rsqrt_fusion) | copy-start | bytes 12292
  354.2 14.2 %copy-start.16 = (bf16[1,1024,2048]{2,1,0:T(8,128)(2,1)S(1)}, bf16[1,1024,2048]{2,1,0:T(8,128)(2,1)}, u32[]{:S(2)}) copy-start(bf16[1,1024,2048]{2,1,0:T(8,128)(2,1)} %param.18) | copy-start | bytes 12582916
  354.2 14.2 %copy-start.34 = (f32[1024]{0:T(1024)S(1)}, f32[1024]{0:T(1024)}, u32[]{:S(2)}) copy-start(f32[1024]{0:T(1024)} %select_reduce_fusion) | copy-start | bytes 12292
  379.5 18.0 %copy-start.52 = (bf16[1024,1024]{1,0:T(8,128)(2,1)}, bf16[1024,1024]{1,0:T(8,128)(2,1)S(1)}, u32[]{:S(2)}) copy-start(bf16[1024,1024]{1,0:T(8,128)(2,1)S(1)} %get-tuple-element.131) | copy-start | bytes 6291460
  406.3 10.0 copy-start.3
  417.4 40.0 %copy-start.14 = (bf16[512,1024]{0,1:T(8,128)(2,1)}, bf16[512,1024]{0,1:T(8,128)(2,1)S(1)}, u32[]{:S(2)}) copy-start(bf16[512,1024]{0,1:T(8,128)(2,1)S(1)} %get-tuple-element.145) | copy-start | bytes 3145732
  433.4 24.0 %copy-start.25 = (f32[4,4,512]{2,1,0:T(4,128)S(1)}, f32[4,4,512]{2,1,0:T(4,128)}, u32[]{:S(2)}) copy-start(f32[4,4,512]{2,1,0:T(4,128)} %copy-done.24) | copy-start | bytes 98308
  433.4 24.0 %copy-start.27 = (f32[4,4,512]{2,1,0:T(4,128)S(1)}, f32[4,4,512]{2,1,0:T(4,128)}, u32[]{:S(2)}) copy-start(f32[4,4,512]{2,1,0:T(4,128)} %copy-done.26) | copy-start | bytes 98308
  433.4 24.0 %copy-start.2 = (pred[512,1024]{0,1:T(8,128)(4,1)S(1)}, pred[512,1024]{0,1:T(8,128)(4,1)}, u32[]{:S(2)}) copy-start(pred[512,1024]{0,1:T(8,128)(4,1)} %copy-done.1) | copy-start | bytes 1572868
  481.1 55.7 %copy-start.12 = (bf16[512,1024]{0,1:T(8,128)(2,1)S(1)}, bf16[512,1024]{0,1:T(8,128)(2,1)}, u32[]{:S(2)}) copy-start(bf16[512,1024]{0,1:T(8,128)(2,1)} %copy.136) | copy-start | bytes 3145732
  536.8 11.0 copy-start.9
  547.7 9.9 copy-start.48
  547.8 9.9 copy-start.49
  557.7 9.5 copy-start.15
  583.4 9.8 copy-start.11
  593.2 10.9 copy-start.35
  604.1 10.2 copy-start.22
  604.1 9.9 copy-start.40
  604.1 9.9 copy-start.18
  604.2 9.9 copy-start.19
  604.2 10.2 copy-start.6
  604.2 10.2 copy-start.29
  604.2 10.2 copy-start.39
  604.2 10.2 copy-start.50
  614.4 15.7 %copy-start.20 = (bf16[1024,4,4,64]{0,3,2,1:T(8,128)(2,1)}, bf16[1024,4,4,64]{0,3,2,1:T(8,128)(2,1)S(1)}, u32[]{:S(2)}) copy-start(bf16[1024,4,4,64]{0,3,2,1:T(8,128)(2,1)S(1)} %pad_maximum_fusion.7) | copy-start | bytes 6291460
  631.2 212.2 %reduce-scatter.8.cloned.1.call-start = ((), (), s32[]{:S(2)}) async-start(), calls=%async_computation.6 | async-start | bytes 9437184 | tf_op jit(solution)/shard_map/reduce_scatter | solution.py:226
  638.7 0.7 copy-start.31
  638.7 0.7 copy-start.37
  638.7 14.0 %copy-start.23 = (bf16[4,64,1024]{2,1,0:T(8,128)(2,1)S(1)}, bf16[4,64,1024]{2,1,0:T(8,128)(2,1)}, u32[]{:S(2)}) copy-start(bf16[4,64,1024]{2,1,0:T(8,128)(2,1)} %copy-done.22) | copy-start | bytes 1572868
  638.7 444.1 %reduce-scatter.6.cloned.1.call-start = ((), (), s32[]{:S(2)}) async-start(), calls=%async_computation.5 | async-start | bytes 16515072 | tf_op jit(solution)/shard_map/reduce_scatter | solution.py:223
  639.4 13.3 %copy-start.7 = (bf16[1,1024,2048]{2,1,0:T(8,128)(2,1)S(1)}, bf16[1,1024,2048]{2,1,0:T(8,128)(2,1)}, u32[]{:S(2)}) copy-start(bf16[1,1024,2048]{2,1,0:T(8,128)(2,1)} %param.17) | copy-start | bytes 12582916
  678.2 477.0 %all-reduce.3.cloned.1.call-start = ((), (), s32[]{:S(2)}) async-start(), calls=%async_computation.8 | async-start | bytes 5767168 | tf_op jit(solution)/shard_map/psum | solution.py:243
  699.0 11.1 copy-start.51
  710.1 10.7 copy-start.33
  710.1 10.7 copy-start.42
  710.2 10.7 copy-start.43
  710.2 18.4 %copy-start.44 = (f32[2,256]{1,0:T(2,128)S(1)}, f32[2,256]{1,0:T(2,128)}, u32[]{:S(2)}) copy-start(f32[2,256]{1,0:T(2,128)} %param.33) | copy-start | bytes 6148
  710.2 133.2 %copy-start.5 = (f32[2,128,2048]{2,1,0:T(8,128)S(1)}, f32[2,128,2048]{2,1,0:T(8,128)}, u32[]{:S(2)}) copy-start(f32[2,128,2048]{2,1,0:T(8,128)} %param.23) | copy-start | bytes 6291460
  849.7 241.9 %copy-start.17 = (bf16[2,128,2048]{2,1,0:T(8,128)(2,1)S(1)}, bf16[2,128,2048]{2,1,0:T(8,128)(2,1)}, u32[]{:S(2)}) copy-start(bf16[2,128,2048]{2,1,0:T(8,128)(2,1)} %reduce-scatter.8.cloned.1.call-done) | copy-start | bytes 3145732
  1174.6 9.0 copy-start.21
Sparse Core Ops, SparseCore 0:
  11.0 204.6 all-gather.2
  218.5 123.0 all-gather.4
  631.3 60.0 reduce-scatter.9
  695.3 148.0 reduce-scatter.7
  846.9 235.8 reduce-scatter.5
  1091.6 63.4 all-reduce.2
where the time goes:
time: 1200 us
  waiting for transfers between devices  588 us (49%)
  matrix products  320 us (27%)
  other arithmetic  169 us (14%)
  local copies, waits for them, and re-layouts  75.2 us (6%)
  blocking collectives  29 us (2%)
  between operations  15.1 us (1%)
    reduce_scatter x1, waiting for transfers between devices, body(): lax.psum_scatter(grad_in_full.astype(jnp.bfloat16), 'fsdp', scatter_dimen...  233 us
    all_gather x1, waiting for transfers between devices, body(): lax.all_gather(w_in.astype(jnp.bfloat16), 'fsdp', axis=0, tiled=True)  175 us
    reduce_scatter x1, waiting for transfers between devices, body(): lax.psum_scatter(grad_out_full.astype(jnp.bfloat16), 'fsdp', scatter_dime...  114 us
    unnamed x119, local copies, waits for them, and re-layouts  67 us
    convert_element_type x1, other arithmetic, body(): d_scores = (attn_probs * (d_probs - inner)).astype(jnp.bfloat16)  55.6 us
    dot_general x2, matrix products, body(): jnp.einsum('qkgd,skd->kgqs', block_grad, value_heads, preferred_element_t...  47.7 us
    psum x1, waiting for transfers between devices, body(): lax.psum(delta_in.astype(jnp.bfloat16), 'rep').astype(jnp.float32)  43 us
    dot_general x2, matrix products, body(): jnp.einsum('kgqs,qkgd->skd', probs_low, block_grad, preferred_element_typ...  32.2 us
  transfers between devices with their start and end apart: 6, of which 5 were waited for; matrix products, arithmetic and copies ran while one was open for 19% of the time, Pallas kernels for 0%

commit v1 on v0

v1 whole, which is shorter than its diff:
```python
import functools
import jax
import jax.numpy as jnp
from jax import lax
from jax.experimental import pallas as pl
from jax.experimental.pallas import tpu as pltpu
from jax.sharding import PartitionSpec as P

H = 16
HD = 64
KVH = 4
FF = 1024
LEN = 1024
NCORP = 8
f32 = jnp.float32
bf16 = jnp.bfloat16
norm_eps = 1e-06
BQ = 256
NT = (((1,), (1,)), ((), ()))
TN = (((0,), (0,)), ((), ()))


def mm(a, b, dims=(((1,), (0,)), ((), ()))):
    return lax.dot_general(a, b, dims, preferred_element_type=f32)


def params(**kw):
    return pltpu.CompilerParams(vmem_limit_bytes=60 << 20, **kw)


def one(shape, index):
    return pl.BlockSpec(shape, index, pipeline_mode=pl.Buffered(1))


def qkv_kernel(x_ref, g_ref, w_ref, first_ref, packed_ref):
    x = x_ref[...].astype(f32)
    r = lax.rsqrt(jnp.mean(x * x, axis=-1, keepdims=True) + norm_eps)
    first = (x * r * g_ref[0:1, :]).astype(bf16)
    first_ref[...] = first
    packed_ref[...] = mm(first, w_ref[...]).astype(bf16)


def qkv(x, gains, w):
    rows, width = x.shape
    cols = w.shape[1]
    return pl.pallas_call(
        qkv_kernel,
        grid=(rows // BQ,),
        in_specs=[
            pl.BlockSpec((BQ, width), lambda i: (i, 0)),
            one(gains.shape, lambda i: (0, 0)),
            one((width, cols), lambda i: (0, 0)),
        ],
        out_specs=[
            pl.BlockSpec((BQ, width), lambda i: (i, 0)),
            pl.BlockSpec((BQ, cols), lambda i: (i, 0)),
        ],
        out_shape=[
            jax.ShapeDtypeStruct((rows, width), bf16),
            jax.ShapeDtypeStruct((rows, cols), bf16),
        ],
        compiler_params=params(),
        cost_estimate=pl.CostEstimate(
            flops=2 * rows * width * cols, bytes_accessed=rows * width * 4 + width * cols * 2, transcendentals=0
        ),
        name="norm_qkv",
    )(x, gains, w)


def doc_start(lengths_ref, position):
    end = jnp.int32(0)
    start = jnp.zeros_like(position)
    for j in range(lengths_ref.shape[0]):
        end = end + lengths_ref[j]
        start = jnp.where(position >= end, end, start)
    return start


def key_blocks(lengths_ref, i):
    first_row = i * BQ
    return i + 1 - doc_start(lengths_ref, first_row) // BQ


def max_blocks():
    return LEN // (2 * BQ) + 1


def attn_kernel(len_ref, q_ref, k_ref, v_ref, o_ref, lse_ref):
    i = pl.program_id(0)
    count = key_blocks(len_ref, i)
    row = i * BQ + lax.broadcasted_iota(jnp.int32, (BQ, 1), 0)
    start = doc_start(len_ref, row)
    lane = lax.broadcasted_iota(jnp.int32, (BQ, 128), 1)
    for nb in range(1, max_blocks() + 1):

        @pl.when(count == nb)
        def _():
            span = nb * BQ
            base = pl.multiple_of((i - (nb - 1)) * BQ, BQ)
            col = base + lax.broadcasted_iota(jnp.int32, (BQ, span), 1)
            bias = jnp.where((col >= start) & (col <= row), 0.0, -1e30)
            k2 = k_ref[pl.ds(base, span), :]
            v2 = v_ref[pl.ds(base, span), :]
            tile = jnp.zeros((BQ, 128), f32)
            outs = []
            for kv in range(2):
                k = k2[:, kv * HD : (kv + 1) * HD]
                v = v2[:, kv * HD : (kv + 1) * HD]
                for g in range(H // KVH):
                    h = kv * (H // KVH) + g
                    q = q_ref[:, h * HD : (h + 1) * HD] * jnp.asarray(HD**-0.5, bf16)
                    s = mm(q, k, NT) + bias
                    m = jnp.max(s, axis=-1, keepdims=True)
                    e = jnp.exp(s - m)
                    total = jnp.sum(e, axis=-1, keepdims=True)
                    o = mm(e.astype(bf16), v) * (1.0 / total)
                    outs.append(o.astype(bf16))
                    tile = jnp.where(lane == h, m + jnp.log(total), tile)
            o_ref[...] = jnp.concatenate(outs, axis=1)
            lse_ref[...] = tile.T[0:8, :]


def attention(lengths, packed):
    qw = H // 2 * HD
    kcol = H * HD // 128
    vcol = kcol + KVH * HD // 128
    return pl.pallas_call(
        attn_kernel,
        grid_spec=pltpu.PrefetchScalarGridSpec(
            num_scalar_prefetch=1,
            grid=(LEN // BQ, 2),
            in_specs=[
                pl.BlockSpec((BQ, qw), lambda i, p, s: (i, p)),
                pl.BlockSpec((LEN, 128), lambda i, p, s: (0, kcol + p)),
                pl.BlockSpec((LEN, 128), lambda i, p, s: (0, vcol + p)),
            ],
            out_specs=[
                pl.BlockSpec((BQ, qw), lambda i, p, s: (i, p)),
                pl.BlockSpec((8, BQ), lambda i, p, s: (p, i)),
            ],
        ),
        out_shape=[
            jax.ShapeDtypeStruct((LEN, H * HD), bf16),
            jax.ShapeDtypeStruct((H, LEN), f32),
        ],
        compiler_params=params(),
        cost_estimate=pl.CostEstimate(flops=4 * H * LEN * LEN * HD * 4, bytes_accessed=1 << 24, transcendentals=0),
        name="attention",
    )(lengths, packed, packed, packed)


def attn_back_kernel(len_ref, q_ref, k_ref, v_ref, d_ref, o_ref, lse_ref, dq_ref, dk_ref, dv_ref, dk_acc, dv_acc):
    i = pl.program_id(1)
    count = key_blocks(len_ref, i)
    row = i * BQ + lax.broadcasted_iota(jnp.int32, (1, BQ), 1)
    start = doc_start(len_ref, row)
    lane = lax.broadcasted_iota(jnp.int32, (BQ, 128), 1)
    group = H // KVH
    scale = jnp.asarray(HD**-0.5, bf16)

    @pl.when(i == 0)
    def _():
        dk_acc[...] = jnp.zeros_like(dk_acc)
        dv_acc[...] = jnp.zeros_like(dv_acc)

    tile = jnp.zeros((BQ, 128), f32)
    for h in range(2 * group):
        cols = slice(h * HD, (h + 1) * HD)
        dot = jnp.sum(d_ref[:, cols].astype(f32) * o_ref[:, cols].astype(f32), axis=-1, keepdims=True)
        tile = jnp.where(lane == h, dot, tile)
    inner = tile.T
    for nb in range(1, max_blocks() + 1):

        @pl.when(count == nb)
        def _():
            span = nb * BQ
            base = pl.multiple_of((i - (nb - 1)) * BQ, BQ)
            key = base + lax.broadcasted_iota(jnp.int32, (span, BQ), 0)
            bias = jnp.where((key >= start) & (key <= row), 0.0, -1e30)
            k2 = k_ref[pl.ds(base, span), :]
            v2 = v_ref[pl.ds(base, span), :]
            dks, dvs = [], []
            for kv in range(2):
                k = k2[:, kv * HD : (kv + 1) * HD]
                v = v2[:, kv * HD : (kv + 1) * HD]
                dk = dv = None
                dqs = []
                for g in range(group):
                    h = kv * group + g
                    cols = slice(h * HD, (h + 1) * HD)
                    q = q_ref[:, cols] * scale
                    d = d_ref[:, cols]
                    s = mm(k, q, NT) + bias
                    p = jnp.exp(s - lse_ref[h : h + 1, :])
                    dp = mm(v, d, NT)
                    ds = (p * (dp - inner[h : h + 1, :])).astype(bf16)
                    dv_h = mm(p.astype(bf16), d)
                    dk_h = mm(ds, q)
                    dv = dv_h if dv is None else dv + dv_h
                    dk = dk_h if dk is None else dk + dk_h
                    dqs.append(mm(k, ds, TN))
                dq = jnp.concatenate(dqs, axis=0) * (HD**-0.5)
                dq_ref[:, kv * group * HD : (kv + 1) * group * HD] = dq.T.astype(bf16)
                dks.append(dk)
                dvs.append(dv)
            dk_acc[pl.ds(base, span), :] += jnp.concatenate(dks, axis=1)
            dv_acc[pl.ds(base, span), :] += jnp.concatenate(dvs, axis=1)

    @pl.when(i == pl.num_programs(1) - 1)
    def _():
        dk_ref[...] = dk_acc[...].astype(bf16)
        dv_ref[...] = dv_acc[...].astype(bf16)


def attention_back(lengths, packed, d_mixed, mixed, lse):
    qw = H // 2 * HD
    kcol = H * HD // 128
    vcol = kcol + KVH * HD // 128
    return pl.pallas_call(
        attn_back_kernel,
        grid_spec=pltpu.PrefetchScalarGridSpec(
            num_scalar_prefetch=1,
            grid=(2, LEN // BQ),
            in_specs=[
                pl.BlockSpec((BQ, qw), lambda p, i, s: (i, p)),
                pl.BlockSpec((LEN, 128), lambda p, i, s: (0, kcol + p)),
                pl.BlockSpec((LEN, 128), lambda p, i, s: (0, vcol + p)),
                pl.BlockSpec((BQ, qw), lambda p, i, s: (i, p)),
                pl.BlockSpec((BQ, qw), lambda p, i, s: (i, p)),
                pl.BlockSpec((8, BQ), lambda p, i, s: (p, i)),
            ],
            out_specs=[
                pl.BlockSpec((BQ, qw), lambda p, i, s: (i, p)),
                pl.BlockSpec((LEN, 128), lambda p, i, s: (0, p)),
                pl.BlockSpec((LEN, 128), lambda p, i, s: (0, p)),
            ],
            scratch_shapes=[pltpu.VMEM((LEN, 128), f32), pltpu.VMEM((LEN, 128), f32)],
        ),
        out_shape=[
            jax.ShapeDtypeStruct((LEN, H * HD), bf16),
            jax.ShapeDtypeStruct((LEN, KVH * HD), bf16),
            jax.ShapeDtypeStruct((LEN, KVH * HD), bf16),
        ],
        compiler_params=params(),
        cost_estimate=pl.CostEstimate(flops=10 * H * LEN * LEN * HD * 4, bytes_accessed=1 << 24, transcendentals=0),
        name="attention_back",
    )(lengths, packed, packed, packed, d_mixed, mixed, lse)


def token_weight(table_ref, ids):
    weight = jnp.zeros(ids.shape, f32)
    for j in range(table_ref.shape[0]):
        weight = jnp.where(ids == j, table_ref[j].astype(f32) * 0.25, weight)
    return weight


def ffn_kernel(table_ref, x_ref, mixed_ref, t_ref, ids_ref, g_ref, proj_ref, wf_ref, down_ref,
               middle_ref, second_ref, hidden_ref, dboth_ref, dy_ref):
    middle = x_ref[...].astype(f32) + mm(mixed_ref[...], proj_ref[...])
    middle_ref[...] = middle
    r = lax.rsqrt(jnp.mean(middle * middle, axis=-1, keepdims=True) + norm_eps)
    second = (middle * r * g_ref[1:2, :]).astype(bf16)
    second_ref[...] = second
    dy = (token_weight(table_ref, ids_ref[...]) * t_ref[...].astype(f32)).astype(bf16)
    dy_ref[...] = dy
    step = 512
    for c in range(0, FF, step):
        gate = mm(second, wf_ref[:, c : c + step])
        up = mm(second, wf_ref[:, FF + c : FF + c + step])
        dh = mm(dy, down_ref[c : c + step, :], NT)
        sig = jax.nn.sigmoid(gate)
        silu = gate * sig
        hidden_ref[:, c : c + step] = (silu * up).astype(bf16)
        dboth_ref[:, c : c + step] = (dh * up * sig * (1.0 + gate * (1.0 - sig))).astype(bf16)
        dboth_ref[:, FF + c : FF + c + step] = (dh * silu).astype(bf16)


def ffn(table, x, mixed, target, ids, gains, proj, wf, down):
    width = x.shape[1]
    rowb = lambda n: pl.BlockSpec((BQ, n), lambda i, s: (i, 0))
    whole = lambda a: one(a.shape, lambda i, s: (0, 0))
    return pl.pallas_call(
        ffn_kernel,
        grid_spec=pltpu.PrefetchScalarGridSpec(
            num_scalar_prefetch=1,
            grid=(LEN // BQ,),
            in_specs=[rowb(width), rowb(H * HD), rowb(width), rowb(1), whole(gains), whole(proj), whole(wf), whole(down)],
            out_specs=[rowb(width), rowb(width), rowb(FF), rowb(2 * FF), rowb(width)],
        ),
        out_shape=[
            jax.ShapeDtypeStruct((LEN, width), f32),
            jax.ShapeDtypeStruct((LEN, width), bf16),
            jax.ShapeDtypeStruct((LEN, FF), bf16),
            jax.ShapeDtypeStruct((LEN, 2 * FF), bf16),
            jax.ShapeDtypeStruct((LEN, width), bf16),
        ],
        compiler_params=params(),
        cost_estimate=pl.CostEstimate(flops=2 * LEN * width * FF * 4, bytes_accessed=40 << 20, transcendentals=0),
        name="ffn",
    )(table, x, mixed, target, ids, gains, proj, wf, down)


def mid_kernel(table_ref, middle_ref, hidden_ref, dboth_ref, t_ref, ids_ref, g_ref, proj_ref, wf_ref, down_ref,
               act_ref, dmid_ref, dlow_ref, dmix_ref, gain_ref):
    middle = middle_ref[...]
    act_ref[...] = (middle + mm(hidden_ref[...], down_ref[...])).astype(bf16)
    r = lax.rsqrt(jnp.mean(middle * middle, axis=-1, keepdims=True) + norm_eps)
    n2 = middle * r
    ds2 = mm(dboth_ref[...], wf_ref[...], NT)
    prod = ds2 * n2
    part = jnp.sum(prod.reshape(BQ // 8, 8, prod.shape[1]), axis=0)

    @pl.when(pl.program_id(0) == 0)
    def _():
        gain_ref[...] = jnp.zeros_like(gain_ref)

    gain_ref[...] += part
    g = g_ref[1:2, :]
    e2 = ds2 * g
    dy = token_weight(table_ref, ids_ref[...]) * t_ref[...].astype(f32)
    dmid = dy + r * (e2 - n2 * jnp.mean(prod * g, axis=-1, keepdims=True))
    dmid_ref[...] = dmid
    low = dmid.astype(bf16)
    dlow_ref[...] = low
    dmix_ref[...] = mm(low, proj_ref[...], NT).astype(bf16)


def mid(table, middle, hidden, dboth, target, ids, gains, proj, wf, down):
    width = middle.shape[1]
    rowb = lambda n: pl.BlockSpec((BQ, n), lambda i, s: (i, 0))
    whole = lambda a: one(a.shape, lambda i, s: (0, 0))
    return pl.pallas_call(
        mid_kernel,
        grid_spec=pltpu.PrefetchScalarGridSpec(
            num_scalar_prefetch=1,
            grid=(LEN // BQ,),
            in_specs=[rowb(width), rowb(FF), rowb(2 * FF), rowb(width), rowb(1), whole(gains), whole(proj), whole(wf), whole(down)],
            out_specs=[rowb(width), rowb(width), rowb(width), rowb(H * HD), pl.BlockSpec((8, width), lambda i, s: (0, 0))],
        ),
        out_shape=[
            jax.ShapeDtypeStruct((LEN, width), bf16),
            jax.ShapeDtypeStruct((LEN, width), f32),
            jax.ShapeDtypeStruct((LEN, width), bf16),
            jax.ShapeDtypeStruct((LEN, H * HD), bf16),
            jax.ShapeDtypeStruct((8, width), f32),
        ],
        compiler_params=params(),
        cost_estimate=pl.CostEstimate(flops=2 * LEN * width * FF * 4, bytes_accessed=40 << 20, transcendentals=0),
        name="mid",
    )(table, middle, hidden, dboth, target, ids, gains, proj, wf, down)


def input_kernel(x_ref, dmid_ref, dq_ref, dk_ref, dv_ref, g_ref, w_ref, out_ref, gain_ref):
    x = x_ref[...].astype(f32)
    r = lax.rsqrt(jnp.mean(x * x, axis=-1, keepdims=True) + norm_eps)
    n1 = x * r
    q, k = H * HD, H * HD + KVH * HD
    ds1 = mm(dq_ref[...], w_ref[:, :q], NT) + mm(dk_ref[...], w_ref[:, q:k], NT) + mm(dv_ref[...], w_ref[:, k:], NT)
    prod = ds1 * n1
    part = jnp.sum(prod.reshape(BQ // 8, 8, prod.shape[1]), axis=0)

    @pl.when(pl.program_id(0) == 0)
    def _():
        gain_ref[...] = jnp.zeros_like(gain_ref)

    gain_ref[...] += part
    g = g_ref[0:1, :]
    out = dmid_ref[...] + r * (ds1 * g - n1 * jnp.mean(prod * g, axis=-1, keepdims=True))
    out_ref[...] = out.astype(bf16)


def input_back(x, dmid, dq, dk, dv, gains, w):
    width = x.shape[1]
    rowb = lambda n: pl.BlockSpec((BQ, n), lambda i: (i, 0))
    whole = lambda a: one(a.shape, lambda i: (0, 0))
    return pl.pallas_call(
        input_kernel,
        grid=(LEN // BQ,),
        in_specs=[rowb(width), rowb(width), rowb(H * HD), rowb(KVH * HD), rowb(KVH * HD), whole(gains), whole(w)],
        out_specs=[rowb(width), pl.BlockSpec((8, width), lambda i: (0, 0))],
        out_shape=[jax.ShapeDtypeStruct((LEN, width), bf16), jax.ShapeDtypeStruct((8, width), f32)],
        compiler_params=params(),
        cost_estimate=pl.CostEstimate(flops=2 * LEN * width * 1536, bytes_accessed=24 << 20, transcendentals=0),
        name="input_back",
    )(x, dmid, dq, dk, dv, gains, w)


def grad_kernel(pick_ref, a_ref, *refs):
    out_ref = refs[-1]
    b_refs = refs[:-1]
    add_ref = None
    if len(b_refs) > 1 and len(b_refs[-1].shape) == 3:
        add_ref, b_refs = b_refs[-1], b_refs[:-1]
    col = 0
    a = a_ref[...]
    for b_ref in b_refs:
        n = b_ref.shape[1]
        g = mm(a, b_ref[...], TN)
        if add_ref is not None:
            g = g + add_ref[0, :, col : col + n].astype(f32)
        out_ref[0, :, col : col + n] = g.astype(bf16)
        col += n


def grad_rows(pick, a, bs, rows, add=None, name="grad"):
    cols = sum(width for _, _, width in bs)
    count = pick.shape[0]
    specs = [pl.BlockSpec((LEN, rows), lambda j, p: (0, p[j]))]
    specs += [one((LEN, width), functools.partial(lambda at, j, p: (0, at), at)) for _, at, width in bs]
    ops = [a, *(b for b, _, _ in bs)]
    if add is not None:
        specs.append(pl.BlockSpec((1, rows, cols), lambda j, p: (j, 0, 0)))
        ops.append(add)
    return pl.pallas_call(
        grad_kernel,
        grid_spec=pltpu.PrefetchScalarGridSpec(
            num_scalar_prefetch=1,
            grid=(count,),
            in_specs=specs,
            out_specs=pl.BlockSpec((1, rows, cols), lambda j, p: (j, 0, 0)),
        ),
        out_shape=jax.ShapeDtypeStruct((count, rows, cols), bf16),
        compiler_params=params(),
        cost_estimate=pl.CostEstimate(flops=2 * LEN * rows * count * cols, bytes_accessed=12 << 20, transcendentals=0),
        name=name,
    )(pick, *ops)


def flip_pairs(n):
    return [(i, i ^ 1) for i in range(n)]


def add_low(a, b):
    return (a.astype(f32) + b.astype(f32)).astype(a.dtype)


def line_sum(blocks, z, line):
    right = left = None
    for step in range(1, line):
        at_right = jnp.clip(line - step + z, 0, line - 1)
        at_left = jnp.clip(z - line + step, 0, line - 1)
        to_right = lax.dynamic_index_in_dim(blocks, at_right, 0, keepdims=False)
        to_left = lax.dynamic_index_in_dim(blocks, at_left, 0, keepdims=False)
        if right is not None:
            to_right = add_low(to_right, right)
            to_left = add_low(to_left, left)
        pairs = [(k * 2 + y, k * 2 + 2 + y) for k in range(step) for y in range(2)]
        last = 2 * line - 1
        right = lax.ppermute(to_right, "fsdp", pairs)
        left = lax.ppermute(to_left, "fsdp", [(last - a, last - b) for a, b in pairs])
    return right, left


beta_first = 0.9
beta_second = 0.95
adam_eps = 1e-08
decay_rate = 0.1
outer_decay = 0.5
outer_rate = 0.7
STEP = 10


def adam_step(grad, first, second, weight, rate):
    first_new = beta_first * first + (1.0 - beta_first) * grad
    second_new = beta_second * second + (1.0 - beta_second) * grad * grad
    ratio = first_new / (1.0 - beta_first**STEP) / (jnp.sqrt(second_new / (1.0 - beta_second**STEP)) + adam_eps)
    local = weight - rate * (ratio + decay_rate * weight)
    return first_new, second_new, weight - local


def outer_step(delta_sum, momentum, weight, groups):
    average = delta_sum / groups
    momentum_new = outer_decay * momentum + average
    return average, momentum_new, weight - outer_rate * (average + outer_decay * momentum_new)


def adam_kernel(place_ref, own_ref, *refs, terms, rate):
    refs = list(refs)
    more = [refs.pop(0) for _ in range(terms)]
    first_ref, second_ref, w_ref = refs[:3]
    grad_ref, first_new_ref, second_new_ref, keep_ref, send_ref = refs[-5:]
    grad = own_ref[0].astype(f32)
    for term in more:
        grad = grad + term[...].astype(f32)
    first_new, second_new, delta = adam_step(grad, first_ref[...], second_ref[...], w_ref[...], rate)
    grad_ref[...] = grad
    first_new_ref[...] = first_new
    second_new_ref[...] = second_new
    half = delta.shape[0] // 2
    low = delta.astype(bf16)
    core = place_ref[1]

    @pl.when(core == 0)
    def _():
        keep_ref[...] = low[:half]
        send_ref[...] = low[half:]

    @pl.when(core != 0)
    def _():
        keep_ref[...] = low[half:]
        send_ref[...] = low[:half]


def adam_piece(place, own, terms, first, second, w, held, rows, row_at, col_at, cols, tile, rate):
    at = lambda j, p: (row_at // rows, col_at // tile + j)
    piece = pl.BlockSpec((rows, tile), lambda j, p: (0, j))
    half = pl.BlockSpec((rows // 2, tile), lambda j, p: (0, j))
    state = pl.BlockSpec((rows, tile), at)
    full = jax.ShapeDtypeStruct(first.shape, f32)
    low = jax.ShapeDtypeStruct((rows // 2, cols), bf16)
    specs = [pl.BlockSpec((1, rows, tile), lambda j, p: (p[0], 0, j))] + [piece] * len(terms) + [state] * 3
    ops = [own, *terms, first, second, w]
    aliases = {}
    if held is not None:
        aliases = {1 + len(ops) + k: k for k in range(3)}
        ops += list(held)
        specs += [pl.BlockSpec(memory_space=pl.ANY)] * 3
    out = pl.pallas_call(
        functools.partial(adam_kernel, terms=len(terms), rate=rate),
        grid_spec=pltpu.PrefetchScalarGridSpec(
            num_scalar_prefetch=1,
            grid=(cols // tile,),
            in_specs=specs,
            out_specs=[state, state, state, half, half],
        ),
        out_shape=[full, full, full, low, low],
        input_output_aliases=aliases,
        compiler_params=params(),
        cost_estimate=pl.CostEstimate(flops=0, bytes_accessed=rows * cols * 28, transcendentals=0),
        name="adam",
    )(place, *ops)
    return out[:3], out[3], out[4]


def outer_kernel(place_ref, keep_ref, other_ref, outer_ref, w_ref, *refs, groups):
    diff_ref, outer_new_ref, new_ref, copy_ref = refs[-4:]
    core = place_ref[1]
    half = keep_ref.shape[0]

    def write(rows, total_ref):
        average, momentum, weight = outer_step(total_ref[...].astype(f32), outer_ref[rows, :], w_ref[rows, :], groups)
        diff_ref[rows, :] = average
        outer_new_ref[rows, :] = momentum
        new_ref[rows, :] = weight
        copy_ref[rows, :] = weight.astype(bf16)

    @pl.when(core == 0)
    def _():
        write(slice(0, half), keep_ref)
        write(slice(half, 2 * half), other_ref)

    @pl.when(core != 0)
    def _():
        write(slice(0, half), other_ref)
        write(slice(half, 2 * half), keep_ref)


def outer_piece(place, keep, other, outer, w, held, rows, row_at, col_at, cols, tile, groups):
    half = pl.BlockSpec((rows // 2, tile), lambda j, p: (0, j))
    state = pl.BlockSpec((rows, tile), lambda j, p: (row_at // rows, col_at // tile + j))
    full = jax.ShapeDtypeStruct(outer.shape, f32)
    specs = [half, half, state, state]
    ops = [keep, other, outer, w]
    aliases = {}
    if held is not None:
        aliases = {1 + len(ops) + k: k for k in range(4)}
        ops += list(held)
        specs += [pl.BlockSpec(memory_space=pl.ANY)] * 4
    return pl.pallas_call(
        functools.partial(outer_kernel, groups=groups),
        grid_spec=pltpu.PrefetchScalarGridSpec(
            num_scalar_prefetch=1, grid=(cols // tile,), in_specs=specs, out_specs=[state] * 4
        ),
        out_shape=[full, full, full, jax.ShapeDtypeStruct(outer.shape, bf16)],
        input_output_aliases=aliases,
        compiler_params=params(),
        cost_estimate=pl.CostEstimate(flops=0, bytes_accessed=rows * cols * 24, transcendentals=0),
        name="outer",
    )(place, *ops)


def rep_sum(keep, send, rep):
    pair = flip_pairs(rep)
    part = add_low(keep, lax.ppermute(send, "rep", pair))
    for hop in range(1, (rep - 1).bit_length()):
        part = add_low(part, lax.ppermute(part, "rep", [(i, i ^ (1 << hop)) for i in range(rep)]))
    return part, lax.ppermute(part, "rep", pair)


def gather_kernel(*refs, count, line, shares):
    ins, outs = refs[:count], refs[count : 2 * count]
    send, recv, local = refs[2 * count :]
    r, f = lax.axis_index("rep"), lax.axis_index("fsdp")
    x, core, z, y = r // 2, r % 2, f // 2, f % 2
    to_y = (r, f + 1 - 2 * y)
    to_x = (r + 2 - 4 * x, f)
    to_core = (r + 1 - 2 * core, f)
    barrier = pltpu.get_barrier_semaphore()
    greet = lambda to: pl.semaphore_signal(barrier, inc=1, device_id=to, device_id_type=pl.DeviceIdType.MESH)
    for to in (to_y, to_x, to_core):
        greet(to)
    pl.when(z > 0)(lambda: greet((r, f - 2)))
    pl.when(z < line - 1)(lambda: greet((r, f + 2)))
    pl.semaphore_wait(barrier, 3 + jnp.where(z > 0, 1, 0) + jnp.where(z < line - 1, 1, 0))

    def item(side, d):
        return 0 if d == 0 else 2 * d - 1 + (side > 0)

    def exists(side, d):
        return None if d == 0 else (z - d >= 0 if side < 0 else z + d < line)

    def guard(cond, fn):
        if cond is None:
            fn()
        else:
            pl.when(cond)(fn)

    def rows_of(m):
        rows = ins[m].shape[0]
        half = rows // 2
        return half, shares[m]

    def copy(src, dst, stage, m, k, to):
        return pltpu.make_async_remote_copy(
            src_ref=src, dst_ref=dst, send_sem=send.at[stage, m, k], recv_sem=recv.at[stage, m, k],
            device_id=to, device_id_type=pl.DeviceIdType.MESH,
        )

    def portion(m):
        half, bx = rows_of(m)
        return pl.ds(pl.multiple_of(core * half + x * bx, 16), half - bx)

    def line_copy(m, side, d):
        plane = z - (d - 1) if side < 0 else z + (d - 1)
        to = (r, f + 2) if side < 0 else (r, f - 2)
        rows = portion(m)
        dst = outs[m].at[plane * 2 + y, rows, :]
        src = ins[m].at[rows, :] if d == 1 else dst
        return copy(src, dst, 0, m, item(side, d), to)

    def line_arrival(m, side, d):
        plane = z - d if side < 0 else z + d
        dst = outs[m].at[plane * 2 + y, portion(m), :]
        return copy(dst, dst, 0, m, item(side, d), to_y)

    def y_copy(m, side, d):
        plane = z + side * d
        dst = outs[m].at[plane * 2 + y, portion(m), :]
        return copy(ins[m].at[portion(m), :] if d == 0 else dst, dst, 1, m, item(side, d), to_y)

    def x_copy(m, side, d):
        half, bx = rows_of(m)
        rows = pl.ds(pl.multiple_of(core * half + x * (half - bx), 16), bx)
        return both_copy(m, side, d, rows, 2, to_x)

    def core_copy(m, side, d):
        half, _ = rows_of(m)
        rows = pl.ds(pl.multiple_of(core * half, 16), half)
        return both_copy(m, side, d, rows, 3, to_core)

    def both_copy(m, side, d, rows, stage, to):
        if d == 0:
            ref = outs[m].at[pl.ds(z * 2 + 1 - y, 1), rows, :]
        else:
            ref = outs[m].at[pl.ds((z + side * d) * 2, 2), rows, :]
        return copy(ref, ref, stage, m, item(side, d), to)

    sides = lambda d: (1,) if d == 0 else (-1, 1)
    order = []
    for m in range(count):
        blocks = [[(m, s, d) for s in sides(d)] for d in range(line)]
        if m == 0:
            order += blocks[0] + blocks[1]
        else:
            order += blocks[1]
        if m + 1 < count:
            order += [(m + 1, 1, 0)]
        for block in blocks[2:]:
            order += block

    def line_stage(m, side, d):
        if d > 0:
            line_arrival(m, side, d).wait_recv()
        if d == 0:
            pl.when(z < line - 1)(lambda: line_copy(m, -1, 1).start())
            pl.when(z > 0)(lambda: line_copy(m, 1, 1).start())
        elif d < line - 1:
            onward = z < line - 1 if side < 0 else z > 0
            pl.when(onward)(lambda: line_copy(m, side, d + 1).start())
        y_copy(m, side, d).start()

    def y_stage(m, side, d):
        y_copy(m, side, d).wait_recv()
        x_copy(m, side, d).start()

    def x_stage(m, side, d):
        x_copy(m, side, d).wait_recv()
        core_copy(m, side, d).start()

    stages = (line_stage, y_stage, x_stage)
    for m in range(count):
        pltpu.make_async_copy(ins[m], outs[m].at[f], local.at[m]).start()
    for k in range(len(order) + len(stages) - 1):
        for lag, stage in enumerate(stages):
            if 0 <= k - lag < len(order):
                it = order[k - lag]
                guard(exists(*it[1:]), functools.partial(stage, *it))
    for it in order:
        m, side, d = it

        def finish():
            core_copy(m, side, d).wait()
            x_copy(m, side, d).wait_send()
            y_copy(m, side, d).wait_send()

        guard(exists(side, d), finish)
        if d > 0:
            sent = z - (d - 1) >= 0 if side < 0 else z + (d - 1) < line
            onward = z < line - 1 if side < 0 else z > 0
            pl.when(sent & onward)(lambda: line_copy(m, side, d).wait_send())
    for m in range(count):
        pltpu.make_async_copy(ins[m], outs[m].at[f], local.at[m]).wait()


def gather(shards, n, shares):
    count = len(shards)
    items = n - 1
    return pl.pallas_call(
        functools.partial(gather_kernel, count=count, line=n // 2, shares=shares),
        out_shape=[jax.ShapeDtypeStruct((n, *a.shape), a.dtype) for a in shards],
        in_specs=[pl.BlockSpec(memory_space=pl.ANY)] * count,
        out_specs=[pl.BlockSpec(memory_space=pl.ANY)] * count,
        scratch_shapes=[
            pltpu.SemaphoreType.DMA((4, count, items)),
            pltpu.SemaphoreType.DMA((4, count, items)),
            pltpu.SemaphoreType.DMA((count,)),
        ],
        compiler_params=pltpu.CompilerParams(collective_id=0, has_side_effects=True),
        cost_estimate=pl.CostEstimate(flops=0, bytes_accessed=200 << 20, transcendentals=0),
        name="gather",
    )(*shards)


def by_neighbours(n, rep):
    return n == 8 and rep == 4


def all_weights(w_in, w_out, gains, n, rep):
    split = H * HD + 2 * KVH * HD
    low_in, low_out = w_in.astype(bf16), w_out.astype(bf16)
    low_gains = jnp.pad(gains.astype(bf16), ((0, 62), (0, 0)))
    shards = [low_gains, low_in[:, :split], low_out[0], low_in[:, split:], low_out[1]]
    if by_neighbours(n, rep):
        full = gather(shards, n, (16, 48, 16, 48, 32))
    else:
        full = [lax.all_gather(a, "fsdp") for a in shards]
    gain_full = full[0][:, :8].astype(f32).transpose(1, 0, 2).reshape(8, -1)
    return [gain_full] + [a.reshape(-1, a.shape[-1]) for a in full[1:]]


rate_in = 0.02
rate_out = 0.08
rate_gains = 1.2


def body(
    tokens,
    target,
    doc_lengths,
    corpus_ids,
    corpus_weights,
    w_in,
    w_out,
    gains,
    first_in,
    first_out,
    first_gains,
    second_in,
    second_out,
    second_gains,
    outer_in,
    outer_out,
    outer_gains,
):
    n, rep = lax.axis_size("fsdp"), lax.axis_size("rep")
    line = n // 2
    f, r = lax.axis_index("fsdp"), lax.axis_index("rep")
    z, y = f // 2, f % 2
    direct = by_neighbours(n, rep)
    place = jnp.stack([z if direct else 0 * z, r % 2, y if direct else 0 * y]).astype(jnp.int32)
    rows_in, rows_out = w_in.shape[0], w_out.shape[1]
    gain_full, wq, proj, wf, down = all_weights(w_in, w_out, gains, n, rep)
    x, tgt, lengths = tokens[0], target[0], doc_lengths[0]
    ids = corpus_ids[0][:, None]

    first_low, packed = qkv(x, gain_full, wq)
    mixed, lse = attention(lengths, packed)
    middle, second_low, hidden, d_both, dy = ffn(corpus_weights, x, mixed, tgt, ids, gain_full, proj, wf, down)

    every = jnp.arange(line, dtype=jnp.int32)
    ours, theirs = every * 2 + y, every * 2 + 1 - y
    flip = flip_pairs(n)

    def by_library(a, bs, name):
        block = 2 * BQ if a.shape[1] % (2 * BQ) == 0 else BQ
        every_row = jnp.arange(a.shape[1] // block, dtype=jnp.int32)
        total = grad_rows(every_row, a, bs, block, name=name)
        return lax.psum_scatter(total.reshape(a.shape[1], -1), "fsdp", scatter_dimension=0, tiled=True)[None], ()

    def pair_first(a, bs, rows, name):
        if not direct:
            return by_library(a, bs, name)
        away = grad_rows(theirs, a, bs, rows, name=name + "_send")
        came = lax.ppermute(away, "fsdp", flip)
        total = grad_rows(ours, a, bs, rows, add=came, name=name + "_keep")
        return total, line_sum(total, z, line)

    def line_first(a, bs, rows, name):
        if not direct:
            return by_library(a, bs, name)
        total = grad_rows(every, a, bs, 2 * rows, name=name)
        right, left = line_sum(total, z, line)
        mine = lax.dynamic_index_in_dim(total, z, 0, keepdims=False)
        mine = (mine.astype(f32) + right.astype(f32) + left.astype(f32)).astype(bf16).reshape(2, rows, -1)
        came = lax.ppermute(lax.dynamic_index_in_dim(mine, 1 - y, 0, keepdims=False), "fsdp", flip)
        return mine, (came,)

    gate_sum = pair_first(second_low, [(d_both, 0, FF)], rows_in, "grad_gate")
    down_sum = line_first(hidden, [(dy, 0, dy.shape[1])], rows_out, "grad_down")
    up_sum = pair_first(second_low, [(d_both, 1, FF)], rows_in, "grad_up")
    activations, d_mid, d_low, d_mix, gain_two = mid(
        corpus_weights, middle, hidden, d_both, tgt, ids, gain_full, proj, wf, down
    )
    proj_sum = pair_first(mixed, [(d_low, 0, d_low.shape[1])], rows_out, "grad_proj")
    dq, dk, dv = attention_back(lengths, packed, d_mix, mixed, lse)
    q_sum = pair_first(first_low, [(dq, 0, H * HD)], rows_in, "grad_q")
    kv_sum = pair_first(first_low, [(dk, 0, KVH * HD), (dv, 0, KVH * HD)], rows_in, "grad_kv")
    input_grad, gain_one = input_back(x, d_mid, dq, dk, dv, gain_full, wq)

    by_y = place.at[0].set(place[2])
    flat = lambda a: a.reshape(-1, a.shape[-1])

    def weight_steps(pieces, first, second, w, outer, rate):
        grads = steps = None
        for spot, ((own, terms), rows, row_at, col_at, cols, tile) in pieces:
            grads, keep, send = adam_piece(
                spot, own, terms, first, second, w, grads, rows, row_at, col_at, cols, tile, rate
            )
            keep, other = rep_sum(keep, send, rep)
            steps = outer_piece(place, keep, other, outer, w, steps, rows, row_at, col_at, cols, tile, rep)
        return grads, steps

    qw, kvw = H * HD, 2 * KVH * HD
    in_pieces = [
        (place, (gate_sum, rows_in, 0, qw + kvw, FF, 512)),
        (place, (up_sum, rows_in, 0, qw + kvw + FF, FF, 512)),
        (place, (q_sum, rows_in, 0, 0, qw, 512)),
        (place, (kv_sum, rows_in, 0, qw, kvw, 512)),
    ]
    width = w_out.shape[2]
    out_pieces = [
        (by_y, (down_sum, rows_out, rows_out, 0, width, 512)),
        (place, (proj_sum, rows_out, 0, 0, width, 512)),
    ]
    out_grads, out_steps = weight_steps(
        out_pieces, flat(first_out[0]), flat(second_out[0]), flat(w_out), flat(outer_out), rate_out
    )
    in_grads, in_steps = weight_steps(in_pieces, first_in[0], second_in[0], w_in, outer_in, rate_in)

    gain_full = jnp.stack([jnp.sum(gain_one, axis=0), jnp.sum(gain_two, axis=0)])
    gain_share = lax.psum_scatter(gain_full, "fsdp", scatter_dimension=1, tiled=True)
    first_gains_new, second_gains_new, delta = adam_step(gain_share, first_gains[0], second_gains[0], gains, rate_gains)
    sum_gains = lax.psum(delta, "rep")
    diff_gains, outer_gains_new, new_gains = outer_step(sum_gains, outer_gains, gains, rep)

    out_shape = lambda a: a.reshape(2, rows_out, width)
    diff_in, outer_in_new, new_in, copy_in = in_steps
    diff_out, outer_out_new, new_out, copy_out = (out_shape(a) for a in out_steps)
    grad_in, first_in_new, second_in_new = in_grads
    grad_out, first_out_new, second_out_new = (out_shape(a) for a in out_grads)
    return (
        activations[None],
        input_grad[None],
        grad_in[None],
        grad_out[None],
        gain_share[None],
        first_in_new[None],
        first_out_new[None],
        first_gains_new[None],
        second_in_new[None],
        second_out_new[None],
        second_gains_new[None],
        diff_in,
        diff_out,
        diff_gains,
        outer_in_new,
        outer_out_new,
        outer_gains_new,
        new_in,
        new_out,
        new_gains,
        copy_in,
        copy_out,
        new_gains.astype(bf16),
    )


def solution(mesh):
    rows = P(("rep", "fsdp"), None, None)
    pair = P(("rep", "fsdp"), None)
    w_in, w_out, gains = P("fsdp", None), P(None, "fsdp", None), P(None, "fsdp")
    m_in, m_out, m_gains = P("rep", "fsdp", None), P("rep", None, "fsdp", None), P("rep", None, "fsdp")
    weights, moments = (w_in, w_out, gains), (m_in, m_out, m_gains)
    return jax.shard_map(
        body,
        mesh=mesh,
        in_specs=(rows, rows, pair, pair, P(), *weights, *moments, *moments, *weights),
        out_specs=(rows, rows, *moments, *moments, *moments, *weights, *weights, *weights, *weights),
        check_vma=False,
    )
```

time: 1200 us -> 825 us (0.69)
  waiting for transfers between devices: 588 us -> 134 us
  Pallas kernels: 0 us -> 423 us
  matrix products: 320 us -> 0 us
  starting transfers between devices: 0.25 us -> 167 us
  other arithmetic: 169 us -> 40.3 us
  local copies, waits for them, and re-layouts: 75.2 us -> 26.9 us
  blocking collectives: 29 us -> 6.03 us
    pallas_call x0 -> x30, Pallas kernels: none -> 423 us  [the longest x1 147 us: gather(): pl.pallas_call(functools.partial(gather_kernel, count=count, line=n // 2,...]
    reduce_scatter x2 -> x0, waiting for transfers between devices: 347 us -> none  [the longest x1 233 us: body(): lax.psum_scatter(grad_in_full.astype(jnp.bfloat16), 'fsdp', scatter_dimen...]
    dot_general x24 -> x0, matrix products: 320 us -> none  [the longest x2 47.7 us: body(): jnp.einsum('qkgd,skd->kgqs', block_grad, value_heads, preferred_element_t...]
    all_gather x2 -> x0, waiting for transfers between devices: 197 us -> none  [the longest x1 175 us: body(): lax.all_gather(w_in.astype(jnp.bfloat16), 'fsdp', axis=0, tiled=True)]
    ppermute x0 -> x60, starting transfers between devices: none -> 167 us  [the longest x18 125 us: line_sum(): right = lax.ppermute(to_right, 'fsdp', pairs)]
    ppermute x0 -> x60, waiting for transfers between devices: none -> 79.2 us  [the longest x18 34.6 us: line_sum(): right = lax.ppermute(to_right, 'fsdp', pairs)]
    unnamed x119 -> x101, local copies, waits for them, and re-layouts: 67 us -> 9.85 us
    convert_element_type x10 -> x35, other arithmetic: 91 us -> 36.3 us  [the longest x30 30.9 us: add_low(): return (a.astype(f32) + b.astype(f32)).astype(a.dtype)]
  transfers between devices with their start and end apart: 6 -> 61, of which waited for: 5 -> 11; matrix products, arithmetic and copies ran while one was open for 19% -> 6% of each run, Pallas kernels for 0% -> 17%
where the time goes in v1:
time: 825 us; the launch traced here: 813 us
  Pallas kernels  423 us (51%)
  starting transfers between devices  167 us (20%)
  waiting for transfers between devices  134 us (16%)
  other arithmetic  40.3 us (5%)
  local copies, waits for them, and re-layouts  26.9 us (3%)
  between operations  15.6 us (2%)
    pallas_call x1, Pallas kernels, gather(): pl.pallas_call(functools.partial(gather_kernel, count=count, line=n // 2,...  147 us
    ppermute x18, starting transfers between devices, line_sum(): right = lax.ppermute(to_right, 'fsdp', pairs)  125 us
    pallas_call x11, Pallas kernels, grad_rows(): pl.pallas_call(grad_kernel, grid_spec=pltpu.PrefetchScalarGridSpec(num_sc...  77.5 us
    unnamed x2, waiting for transfers between devices  54.4 us
    ppermute x18, waiting for transfers between devices, line_sum(): right = lax.ppermute(to_right, 'fsdp', pairs)  34.6 us
    pallas_call x1, Pallas kernels, attention_back(): pl.pallas_call(attn_back_kernel, grid_spec=pltpu.PrefetchScalarGridSpec(n...  31.4 us
    pallas_call x1, Pallas kernels, mid(): pl.pallas_call(mid_kernel, grid_spec=pltpu.PrefetchScalarGridSpec(num_sca...  31.1 us
    convert_element_type x30, other arithmetic, add_low(): return (a.astype(f32) + b.astype(f32)).astype(a.dtype)  30.9 us
  transfers between devices with their start and end apart: 61, of which 11 were waited for; matrix products, arithmetic and copies ran while one was open for 6% of the time, Pallas kernels for 17%

profile of v1, /device:TPU:0, one launch (start us, length us, event | category | flops | bytes accessed | tf_op | source)
XLA Modules:
  0.0 812.8 jit_solution(18426095199153797080)
XLA Ops:
  7.2 2.2 convert_element_type.427
  13.3 147.4 %gather.1 = (bf16[8,64,256]{2,1,0:T(8,128)(2,1)}, bf16[8,256,1536]{2,1,0:T(8,128)(2,1)}, bf16[8,128,2048]{2,1,0:T(8,128)(2,1)}, bf16[8,256,2048]{2,1,0:T(8,128)(2,1)}, bf16[8,128,2048]{2,1,0:T(8,128)(2,1)}) custom-call(bf16[64,256]{1,0:T(8,128)(2,1)} %pad.6.refs_0_, bf16[256,1536]{1,0:T(8,128)(2,1)} %slice.30.refs_1_, ...), custom_call_target="tpu_custom_call" | custom-call | bytes 209715200 | tf_op jit(solution)/shard_map/gather/pallas_call | solution.py:728
  163.7 12.3 %norm_qkv.1 = (bf16[1024,2048]{1,0:T(8,128)(2,1)}, bf16[1024,1536]{1,0:T(8,128)(2,1)}) custom-call(bf16[1024,2048]{1,0:T(8,128)(2,1)} %bitcast.205, f32[8,2048]{1,0:T(8,128)} %bitcast.191, bf16[2048,1536]{1,0:T(8,128)(2,1)} %bitcast.201), custom_call_target="tpu_custom_call" | custom-call | flops 6442450944 | bytes 14680064 | tf_op jit(solution)/shard_map/norm_qkv/pallas_call | solution.py:46
  176.0 20.9 %attention.1 = (bf16[1024,1024]{1,0:T(8,128)(2,1)}, f32[16,1024]{1,0:T(8,128)}) custom-call(s32[4]{0:T(128)} %bitcast.212, bf16[1024,1536]{1,0:T(8,128)(2,1)} %get-tuple-element.115.q_ref.k_ref.v_ref, bf16[1024,1536]{1,0:T(8,128)(2,1)} %get-tuple-element.115.q_ref.k_ref.v_ref, bf16[1024,1536]{1,0:T(8,128)(2,1)} %get-tuple-element.115.q_ref.k_ref.v_ref), custom_call_target="tpu_custom_call" | custom-call | flops 17179869184 | bytes 16777216 | tf_op jit(solution)/shard_map/attention/pallas_call | solution.py:127
  196.9 28.9 %ffn.1 = (f32[1024,2048]{1,0:T(8,128)}, bf16[1024,2048]{1,0:T(8,128)(2,1)}, bf16[1024,1024]{1,0:T(8,128)(2,1)}, bf16[1024,2048]{1,0:T(8,128)(2,1)}, bf16[1024,2048]{1,0:T(8,128)(2,1)}) custom-call(s32[8]{0:T(128)} %table_ref.3, bf16[1024,2048]{1,0:T(8,128)(2,1)} %bitcast.206, bf16[1024,1024]{1,0:T(8,128)(2,1)} %get-tuple-element.116.mixed_ref.o_ref.a_ref, ...), custom_call_target="tpu_custom_call" | custom-call | flops 17179869184 | bytes 41943040 | tf_op jit(solution)/shard_map/ffn/pallas_call | solution.py:282
  225.8 31.1 %mid.1 = (bf16[1024,2048]{1,0:T(8,128)(2,1)}, f32[1024,2048]{1,0:T(8,128)}, bf16[1024,2048]{1,0:T(8,128)(2,1)}, bf16[1024,1024]{1,0:T(8,128)(2,1)}, f32[8,2048]{1,0:T(8,128)}) custom-call(s32[8]{0:T(128)} %table_ref.3, f32[1024,2048]{1,0:T(8,128)} %get-tuple-element.120.middle_ref, bf16[1024,1024]{1,0:T(8,128)(2,1)} %get-tuple-element.121.hidden_ref.a_ref, ...), custom_call_target="tpu_custom_call" | custom-call | flops 17179869184 | bytes 41943040 | tf_op jit(solution)/shard_map/mid/pallas_call | solution.py:332
  256.9 31.4 %attention_back.1 = (bf16[1024,1024]{1,0:T(8,128)(2,1)}, bf16[1024,256]{1,0:T(8,128)(2,1)}, bf16[1024,256]{1,0:T(8,128)(2,1)}) custom-call(s32[4]{0:T(128)} %bitcast.213, bf16[1024,1536]{1,0:T(8,128)(2,1)} %get-tuple-element.115.q_ref.k_ref.v_ref, bf16[1024,1536]{1,0:T(8,128)(2,1)} %get-tuple-element.115.q_ref.k_ref.v_ref, ...), custom_call_target="tpu_custom_call" | custom-call | flops 42949672960 | bytes 16777216 | tf_op jit(solution)/shard_map/attention_back/pallas_call | solution.py:219
  288.3 5.5 grad_kv_send.1
  293.7 11.0 %collective-permute-start = (bf16[4,256,512]{2,1,0:T(8,128)(2,1)}, bf16[4,256,512]{2,1,0:T(8,128)(2,1)S(1)}, u32[]{:S(2)}, u32[]{:S(2)}) collective-permute-start(bf16[4,256,512]{2,1,0:T(8,128)(2,1)} %grad_kv_send.1), channel_id=1, source_target_pairs={{0,1},{1,0},{2,3},{3,2},{4,5},{5,4},{6,7},{7,6},{8,9},{9,8},{10,11... | collective-permute-start | bytes 3145736 | tf_op jit(solution)/shard_map/ppermute | solution.py:814
  304.7 6.8 grad_q_send.1
  311.5 6.8 grad_up_send.1
  320.3 7.2 grad_proj_send.1
  328.1 9.6 %grad_down.1 = bf16[4,256,2048]{2,1,0:T(8,128)(2,1)} custom-call(s32[4]{0:T(128)} %iota.8.pick_ref, bf16[1024,1024]{1,0:T(8,128)(2,1)} %get-tuple-element.121.hidden_ref.a_ref, bf16[1024,2048]{1,0:T(8,128)(2,1)} %get-tuple-element.144.refs_0_), custom_call_target="tpu_custom_call" | custom-call | flops 4294967296 | bytes 12582912 | tf_op jit(solution)/shard_map/grad_down/pallas_call | solution.py:414
  337.6 3.1 dynamic-slice_bitcast_fusion.1
  340.7 2.3 collective-permute-start.35
  343.0 17.9 %input_back.1 = (bf16[1024,2048]{1,0:T(8,128)(2,1)}, f32[8,2048]{1,0:T(8,128)}) custom-call(bf16[1024,2048]{1,0:T(8,128)(2,1)} %bitcast.207, f32[1024,2048]{1,0:T(8,128)} %get-tuple-element.124.dmid_ref, bf16[1024,1024]{1,0:T(8,128)(2,1)} %get-tuple-element.127.dq_ref.refs_0_, bf16[1024,256]{1,0:T(8,128)(2,1)} %get-tuple-element.128.dk_ref.refs_0_, ...), custom_call_target="tpu_custom_call" | custom-call | flops 6442450944 | bytes 25165824 | tf_op jit(solution)/shard_map/input_back/pallas_call | solution.py:376
  363.3 5.6 grad_kv_keep.1.own_ref
  373.5 6.9 grad_gate_send.1
  382.5 54.4 %reduce-scatter.4.cloned.1.call-done = f32[256,2]{1,0:T(8,128)} async-done(((f32[2048,2]{1,0:T(8,128)}), f32[256,2]{1,0:T(8,128)}) %reduce-scatter.4.cloned.1.call-update) | async-done | bytes 2064
  440.2 2.9 fusion.2
  444.8 9.0 %collective-permute-start.36 = (bf16[256,2048]{1,0:T(8,128)(2,1)}, bf16[256,2048]{1,0:T(8,128)(2,1)}, u32[]{:S(2)}, u32[]{:S(2)}) collective-permute-start(bf16[256,2048]{1,0:T(8,128)(2,1)} %fusion.2), channel_id=1, source_target_pairs={{0,2},{1,3},{2,4},{3,5},{8,10},{9,11},{10,12},{11,13},{16,18},{17,... | collective-permute-start | bytes 3145736 | tf_op jit(solution)/shard_map/ppermute | solution.py:449
  455.6 7.2 grad_q_keep.1.own_ref
  462.8 2.2 dynamic-slice_bitcast_fusion.9
  466.3 7.2 grad_up_keep.1.own_ref
  473.5 2.2 dynamic-slice_bitcast_fusion.7
  477.9 7.6 grad_proj_keep.1.own_ref
  486.9 2.3 collective-permute-start.15
  489.2 4.4 fusion.3
  494.6 19.8 %collective-permute-done.21.refs_1_ = bf16[4,256,1024]{2,1,0:T(8,128)(2,1)} collective-permute-done((bf16[4,256,1024]{2,1,0:T(8,128)(2,1)}, bf16[4,256,1024]{2,1,0:T(8,128)(2,1)}, u32[]{:S(2)}, u32[]{:S(2)}) %collective-permute-start.21) | collective-permute-done | bytes 2097184 | tf_op jit(solution)/shard_map/ppermute | solution.py:814
  515.9 7.2 grad_gate_keep.1.own_ref
  533.1 2.6 fusion.1
  535.7 18.4 %collective-permute-start.29 = (bf16[128,2048]{1,0:T(8,128)(2,1)S(1)}, bf16[128,2048]{1,0:T(8,128)(2,1)S(1)}, u32[]{:S(2)}, u32[]{:S(2)}) collective-permute-start(bf16[128,2048]{1,0:T(8,128)(2,1)S(1)} %copy-done.19), channel_id=1, source_target_pairs={{0,2},{1,3},{8,10},{9,11},{16,18},{17,19},{24,26},{25,27}} | collective-permute-start | bytes 1572872 | tf_op jit(solution)/shard_map/ppermute | solution.py:449
  557.0 35.5 %collective-permute-start.16 = (bf16[256,1024]{1,0:T(8,128)(2,1)S(1)}, bf16[256,1024]{1,0:T(8,128)(2,1)S(1)}, u32[]{:S(2)}, u32[]{:S(2)}) collective-permute-start(bf16[256,1024]{1,0:T(8,128)(2,1)S(1)} %get-tuple-element.208), channel_id=1, source_target_pairs={{0,2},{1,3},{2,4},{3,5},{8,10},{9,11},{10,12},{11,13},{16,18},{17,... | collective-permute-start | bytes 1572872 | tf_op jit(solution)/shard_map/ppermute | solution.py:449
  593.9 3.9 collective-permute-start.2
  597.9 6.6 collective-permute-start.9
  604.8 5.5 collective-permute-done.2
  613.0 5.7 collective-permute-start.23
  622.4 6.8 collective-permute-done.23
  629.1 5.3 collective-permute-start.30
  635.4 3.6 collective-permute-start.37
  640.3 5.4 collective-permute-start.17
  645.6 9.2 %collective-permute-start.24 = (bf16[256,1024]{1,0:T(8,128)(2,1)}, bf16[256,1024]{1,0:T(8,128)(2,1)}, u32[]{:S(2)}, u32[]{:S(2)}) collective-permute-start(bf16[256,1024]{1,0:T(8,128)(2,1)} %fusion.13), channel_id=1, source_target_pairs={{0,2},{1,3},{2,4},{3,5},{4,6},{5,7},{8,10},{9,11},{10,12},{11,13},... | collective-permute-start | bytes 1572872 | tf_op jit(solution)/shard_map/ppermute | solution.py:449
  655.5 6.0 psum.7
  663.7 3.2 collective-permute-start.10
  667.7 12.3 %collective-permute-done.17.refs_0_ = bf16[256,1024]{1,0:T(8,128)(2,1)} collective-permute-done((bf16[256,1024]{1,0:T(8,128)(2,1)}, bf16[256,1024]{1,0:T(8,128)(2,1)}, u32[]{:S(2)}, u32[]{:S(2)}) %collective-permute-start.17) | collective-permute-done | bytes 524320 | tf_op jit(solution)/shard_map/ppermute | solution.py:449
  681.3 9.9 %collective-permute-done.24.refs_0_ = bf16[256,1024]{1,0:T(8,128)(2,1)} collective-permute-done((bf16[256,1024]{1,0:T(8,128)(2,1)}, bf16[256,1024]{1,0:T(8,128)(2,1)}, u32[]{:S(2)}, u32[]{:S(2)}) %collective-permute-start.24) | collective-permute-done | bytes 524320 | tf_op jit(solution)/shard_map/ppermute | solution.py:449
  691.2 4.4 collective-permute-start.3
  696.8 4.9 adam.6
  701.7 4.9 adam.7
  707.9 4.9 adam.8
  712.8 4.6 collective-permute-start.31
  718.1 4.3 adam.9
  723.0 2.4 fusion.5
  730.7 8.8 %collective-permute-done.41.refs_0_ = bf16[128,2048]{1,0:T(8,128)(2,1)S(1)} collective-permute-done((bf16[128,2048]{1,0:T(8,128)(2,1)S(1)}, bf16[128,2048]{1,0:T(8,128)(2,1)S(1)}, u32[]{:S(2)}, u32[]{:S(2)}) %collective-permute-start.41) | collective-permute-done | bytes 524320 | tf_op jit(solution)/shard_map/ppermute | solution.py:825
  740.3 5.7 adam.10
  748.1 6.0 adam.11
  758.7 7.8 collective-permute-done.55
  767.3 7.0 collective-permute-done.58
  776.7 4.0 outer.6
  781.5 4.0 outer.7
  786.2 4.0 outer.8
  790.9 3.4 outer.9
  795.0 4.9 outer.10
  800.7 4.9 outer.11
  (248 shorter events, 83.4 us)
Async XLA Ops:
  7.2 429.8 %reduce-scatter.4.cloned.1.call-start = ((), (), s32[]{:S(2)}) async-start(), calls=%async_computation.1 | async-start | bytes 1179648
  11.7 150.5 %copy-start.41 = (s32[1,1024]{1,0:T(1,128)S(1)}, s32[1,1024]{1,0:T(1,128)}, u32[]{:S(2)}) copy-start(s32[1,1024]{1,0:T(1,128)} %param.22) | copy-start | bytes 12292
  293.7 68.6 %collective-permute-start = (bf16[4,256,512]{2,1,0:T(8,128)(2,1)}, bf16[4,256,512]{2,1,0:T(8,128)(2,1)S(1)}, u32[]{:S(2)}, u32[]{:S(2)}) collective-permute-start(bf16[4,256,512]{2,1,0:T(8,128)(2,1)} %grad_kv_send.1), channel_id=1, source_target_pairs={{0,1},{1,0},{2,3},{3,2},{4,5},{5,4},{6,7},{7,6},{8,9},{9,8},{10,11... | collective-permute-start | bytes 3145736 | tf_op jit(solution)/shard_map/ppermute | solution.py:814
  311.5 133.3 %collective-permute-start.7 = (bf16[4,256,1024]{2,1,0:T(8,128)(2,1)}, bf16[4,256,1024]{2,1,0:T(8,128)(2,1)}, u32[]{:S(2)}, u32[]{:S(2)}) collective-permute-start(bf16[4,256,1024]{2,1,0:T(8,128)(2,1)} %grad_q_send.1), channel_id=1, source_target_pairs={{0,1},{1,0},{2,3},{3,2},{4,5},{5,4},{6,7},{7,6},{8,9},{9,8},{10,11... | collective-permute-start | bytes 6291464 | tf_op jit(solution)/shard_map/ppermute | solution.py:814
  318.3 146.7 %collective-permute-start.14 = (bf16[4,256,1024]{2,1,0:T(8,128)(2,1)}, bf16[4,256,1024]{2,1,0:T(8,128)(2,1)S(1)}, u32[]{:S(2)}, u32[]{:S(2)}) collective-permute-start(bf16[4,256,1024]{2,1,0:T(8,128)(2,1)} %grad_up_send.1), channel_id=1, source_target_pairs={{0,1},{1,0},{2,3},{3,2},{4,5},{5,4},{6,7},{7,6},{8,9},{9,8},{10,11... | collective-permute-start | bytes 6291464 | tf_op jit(solution)/shard_map/ppermute | solution.py:814
  327.5 148.2 %collective-permute-start.28 = (bf16[4,128,2048]{2,1,0:T(8,128)(2,1)}, bf16[4,128,2048]{2,1,0:T(8,128)(2,1)}, u32[]{:S(2)}, u32[]{:S(2)}) collective-permute-start(bf16[4,128,2048]{2,1,0:T(8,128)(2,1)} %grad_proj_send.1), channel_id=1, source_target_pairs={{0,1},{1,0},{2,3},{3,2},{4,5},{5,4},{6,7},{7,6},{8,9},{9,8},{10,11... | collective-permute-start | bytes 6291464 | tf_op jit(solution)/shard_map/ppermute | solution.py:814
  340.7 98.2 %collective-permute-start.35 = (bf16[256,2048]{1,0:T(8,128)(2,1)}, bf16[256,2048]{1,0:T(8,128)(2,1)}, u32[]{:S(2)}, u32[]{:S(2)}) collective-permute-start(bf16[256,2048]{1,0:T(8,128)(2,1)} %get-tuple-element.197), channel_id=1, source_target_pairs={{0,2},{1,3},{8,10},{9,11},{16,18},{17,19},{24,26},{25,27}} | collective-permute-start | bytes 3145736 | tf_op jit(solution)/shard_map/ppermute | solution.py:449
  370.7 9.7 %collective-permute-start.4 = (bf16[256,512]{1,0:T(8,128)(2,1)}, bf16[256,512]{1,0:T(8,128)(2,1)}, u32[]{:S(2)}, u32[]{:S(2)}) collective-permute-start(bf16[256,512]{1,0:T(8,128)(2,1)} %get-tuple-element.217), channel_id=1, source_target_pairs={{7,5},{6,4},{15,13},{14,12},{23,21},{22,20},{31,29},{30,28}} | collective-permute-start | bytes 786440 | tf_op jit(solution)/shard_map/ppermute | solution.py:450
  380.4 59.1 %collective-permute-start.1 = (bf16[256,512]{1,0:T(8,128)(2,1)S(1)}, bf16[256,512]{1,0:T(8,128)(2,1)}, u32[]{:S(2)}, u32[]{:S(2)}) collective-permute-start(bf16[256,512]{1,0:T(8,128)(2,1)S(1)} %get-tuple-element.218), channel_id=1, source_target_pairs={{0,2},{1,3},{8,10},{9,11},{16,18},{17,19},{24,26},{25,27}} | collective-permute-start | bytes 786440 | tf_op jit(solution)/shard_map/ppermute | solution.py:449
  382.5 73.1 %copy-start.36 = (s32[3]{0:T(128)}, s32[3]{0:T(128)S(1)}, u32[]{:S(2)}) copy-start(s32[3]{0:T(128)S(1)} %pad_add_fusion.place_ref) | copy-start | bytes 40
  437.9 217.0 %copy-start.40 = (f32[2,256]{1,0:T(2,128)}, f32[2,256]{1,0:T(2,128)S(1)}, u32[]{:S(2)}) copy-start(f32[2,256]{1,0:T(2,128)S(1)} %copy.73) | copy-start | bytes 6148
  439.0 75.5 %collective-permute-start.21 = (bf16[4,256,1024]{2,1,0:T(8,128)(2,1)}, bf16[4,256,1024]{2,1,0:T(8,128)(2,1)}, u32[]{:S(2)}, u32[]{:S(2)}) collective-permute-start(bf16[4,256,1024]{2,1,0:T(8,128)(2,1)} %grad_gate_send.1), channel_id=1, source_target_pairs={{0,1},{1,0},{2,3},{3,2},{4,5},{5,4},{6,7},{7,6},{8,9},{9,8},{10,11... | collective-permute-start | bytes 6291464 | tf_op jit(solution)/shard_map/ppermute | solution.py:814
  439.6 3.6 collective-permute-start.5
  443.2 42.3 %collective-permute-start.38 = (bf16[256,2048]{1,0:T(8,128)(2,1)}, bf16[256,2048]{1,0:T(8,128)(2,1)}, u32[]{:S(2)}, u32[]{:S(2)}) collective-permute-start(bf16[256,2048]{1,0:T(8,128)(2,1)} %get-tuple-element.198), channel_id=1, source_target_pairs={{7,5},{6,4},{15,13},{14,12},{23,21},{22,20},{31,29},{30,28}} | collective-permute-start | bytes 3145736 | tf_op jit(solution)/shard_map/ppermute | solution.py:450
  444.8 42.1 %collective-permute-start.36 = (bf16[256,2048]{1,0:T(8,128)(2,1)}, bf16[256,2048]{1,0:T(8,128)(2,1)}, u32[]{:S(2)}, u32[]{:S(2)}) collective-permute-start(bf16[256,2048]{1,0:T(8,128)(2,1)} %fusion.2), channel_id=1, source_target_pairs={{0,2},{1,3},{2,4},{3,5},{8,10},{9,11},{10,12},{11,13},{16,18},{17,... | collective-permute-start | bytes 3145736 | tf_op jit(solution)/shard_map/ppermute | solution.py:449
  465.0 59.4 %collective-permute-start.11 = (bf16[256,1024]{1,0:T(8,128)(2,1)}, bf16[256,1024]{1,0:T(8,128)(2,1)S(1)}, u32[]{:S(2)}, u32[]{:S(2)}) collective-permute-start(bf16[256,1024]{1,0:T(8,128)(2,1)} %get-tuple-element.213), channel_id=1, source_target_pairs={{7,5},{6,4},{15,13},{14,12},{23,21},{22,20},{31,29},{30,28}} | collective-permute-start | bytes 1572872 | tf_op jit(solution)/shard_map/ppermute | solution.py:450
  475.7 80.5 %collective-permute-start.8 = (bf16[256,1024]{1,0:T(8,128)(2,1)}, bf16[256,1024]{1,0:T(8,128)(2,1)}, u32[]{:S(2)}, u32[]{:S(2)}) collective-permute-start(bf16[256,1024]{1,0:T(8,128)(2,1)} %get-tuple-element.214), channel_id=1, source_target_pairs={{0,2},{1,3},{8,10},{9,11},{16,18},{17,19},{24,26},{25,27}} | collective-permute-start | bytes 1572872 | tf_op jit(solution)/shard_map/ppermute | solution.py:449
  485.5 41.1 %collective-permute-start.18 = (bf16[256,1024]{1,0:T(8,128)(2,1)}, bf16[256,1024]{1,0:T(8,128)(2,1)}, u32[]{:S(2)}, u32[]{:S(2)}) collective-permute-start(bf16[256,1024]{1,0:T(8,128)(2,1)} %get-tuple-element.209), channel_id=1, source_target_pairs={{7,5},{6,4},{15,13},{14,12},{23,21},{22,20},{31,29},{30,28}} | collective-permute-start | bytes 1572872 | tf_op jit(solution)/shard_map/ppermute | solution.py:450
  486.9 48.8 %collective-permute-start.15 = (bf16[256,1024]{1,0:T(8,128)(2,1)}, bf16[256,1024]{1,0:T(8,128)(2,1)}, u32[]{:S(2)}, u32[]{:S(2)}) collective-permute-start(bf16[256,1024]{1,0:T(8,128)(2,1)} %get-tuple-element.210), channel_id=1, source_target_pairs={{0,2},{1,3},{8,10},{9,11},{16,18},{17,19},{24,26},{25,27}} | collective-permute-start | bytes 1572872 | tf_op jit(solution)/shard_map/ppermute | solution.py:449
  514.4 14.1 %collective-permute-start.32 = (bf16[128,2048]{1,0:T(8,128)(2,1)}, bf16[128,2048]{1,0:T(8,128)(2,1)}, u32[]{:S(2)}, u32[]{:S(2)}) collective-permute-start(bf16[128,2048]{1,0:T(8,128)(2,1)} %get-tuple-element.201), channel_id=1, source_target_pairs={{7,5},{6,4},{15,13},{14,12},{23,21},{22,20},{31,29},{30,28}} | collective-permute-start | bytes 1572872 | tf_op jit(solution)/shard_map/ppermute | solution.py:450
  524.5 7.7 collective-permute-start.39
  526.6 4.5 collective-permute-start.25
  528.6 65.3 %collective-permute-start.22 = (bf16[256,1024]{1,0:T(8,128)(2,1)S(1)}, bf16[256,1024]{1,0:T(8,128)(2,1)S(1)}, u32[]{:S(2)}, u32[]{:S(2)}) collective-permute-start(bf16[256,1024]{1,0:T(8,128)(2,1)S(1)} %get-tuple-element.206), channel_id=1, source_target_pairs={{0,2},{1,3},{8,10},{9,11},{16,18},{17,19},{24,26},{25,27}} | collective-permute-start | bytes 1572872 | tf_op jit(solution)/shard_map/ppermute | solution.py:449
  531.1 23.0 %collective-permute-start.19 = (bf16[256,1024]{1,0:T(8,128)(2,1)S(1)}, bf16[256,1024]{1,0:T(8,128)(2,1)S(1)}, u32[]{:S(2)}, u32[]{:S(2)}) collective-permute-start(bf16[256,1024]{1,0:T(8,128)(2,1)S(1)} %fusion.14), channel_id=1, source_target_pairs={{7,5},{6,4},{5,3},{4,2},{15,13},{14,12},{13,11},{12,10},{23,21},{2... | collective-permute-start | bytes 1572872 | tf_op jit(solution)/shard_map/ppermute | solution.py:450
  532.2 24.8 %collective-permute-start.12 = (bf16[256,1024]{1,0:T(8,128)(2,1)S(1)}, bf16[256,1024]{1,0:T(8,128)(2,1)S(1)}, u32[]{:S(2)}, u32[]{:S(2)}) collective-permute-start(bf16[256,1024]{1,0:T(8,128)(2,1)S(1)} %fusion.18), channel_id=1, source_target_pairs={{7,5},{6,4},{5,3},{4,2},{15,13},{14,12},{13,11},{12,10},{23,21},{2... | collective-permute-start | bytes 1572872 | tf_op jit(solution)/shard_map/ppermute | solution.py:450
  535.7 76.0 %collective-permute-start.29 = (bf16[128,2048]{1,0:T(8,128)(2,1)S(1)}, bf16[128,2048]{1,0:T(8,128)(2,1)S(1)}, u32[]{:S(2)}, u32[]{:S(2)}) collective-permute-start(bf16[128,2048]{1,0:T(8,128)(2,1)S(1)} %copy-done.19), channel_id=1, source_target_pairs={{0,2},{1,3},{8,10},{9,11},{16,18},{17,19},{24,26},{25,27}} | collective-permute-start | bytes 1572872 | tf_op jit(solution)/shard_map/ppermute | solution.py:449
  554.1 43.8 %collective-permute-start.26 = (bf16[256,1024]{1,0:T(8,128)(2,1)S(1)}, bf16[256,1024]{1,0:T(8,128)(2,1)S(1)}, u32[]{:S(2)}, u32[]{:S(2)}) collective-permute-start(bf16[256,1024]{1,0:T(8,128)(2,1)S(1)} %fusion.10), channel_id=1, source_target_pairs={{7,5},{6,4},{5,3},{4,2},{15,13},{14,12},{13,11},{12,10},{23,21},{2... | collective-permute-start | bytes 1572872 | tf_op jit(solution)/shard_map/ppermute | solution.py:450
  556.3 56.7 %collective-permute-start.33 = (bf16[128,2048]{1,0:T(8,128)(2,1)S(1)}, bf16[128,2048]{1,0:T(8,128)(2,1)S(1)}, u32[]{:S(2)}, u32[]{:S(2)}) collective-permute-start(bf16[128,2048]{1,0:T(8,128)(2,1)S(1)} %fusion.6), channel_id=1, source_target_pairs={{7,5},{6,4},{5,3},{4,2},{15,13},{14,12},{13,11},{12,10},{23,21},{2... | collective-permute-start | bytes 1572872 | tf_op jit(solution)/shard_map/ppermute | solution.py:450
  557.0 61.7 %collective-permute-start.16 = (bf16[256,1024]{1,0:T(8,128)(2,1)S(1)}, bf16[256,1024]{1,0:T(8,128)(2,1)S(1)}, u32[]{:S(2)}, u32[]{:S(2)}) collective-permute-start(bf16[256,1024]{1,0:T(8,128)(2,1)S(1)} %get-tuple-element.208), channel_id=1, source_target_pairs={{0,2},{1,3},{2,4},{3,5},{8,10},{9,11},{10,12},{11,13},{16,18},{17,... | collective-permute-start | bytes 1572872 | tf_op jit(solution)/shard_map/ppermute | solution.py:449
  593.9 16.5 %collective-permute-start.2 = (bf16[256,512]{1,0:T(8,128)(2,1)S(1)}, bf16[256,512]{1,0:T(8,128)(2,1)S(1)}, u32[]{:S(2)}, u32[]{:S(2)}) collective-permute-start(bf16[256,512]{1,0:T(8,128)(2,1)S(1)} %get-tuple-element.216), channel_id=1, source_target_pairs={{0,2},{1,3},{2,4},{3,5},{8,10},{9,11},{10,12},{11,13},{16,18},{17,... | collective-permute-start | bytes 786440 | tf_op jit(solution)/shard_map/ppermute | solution.py:449
  597.9 37.6 %collective-permute-start.9 = (bf16[256,1024]{1,0:T(8,128)(2,1)S(1)}, bf16[256,1024]{1,0:T(8,128)(2,1)}, u32[]{:S(2)}, u32[]{:S(2)}) collective-permute-start(bf16[256,1024]{1,0:T(8,128)(2,1)S(1)} %get-tuple-element.212), channel_id=1, source_target_pairs={{0,2},{1,3},{2,4},{3,5},{8,10},{9,11},{10,12},{11,13},{16,18},{17,... | collective-permute-start | bytes 1572872 | tf_op jit(solution)/shard_map/ppermute | solution.py:449
  610.4 28.6 %collective-permute-start.13 = (bf16[256,1024]{1,0:T(8,128)(2,1)S(1)}, bf16[256,1024]{1,0:T(8,128)(2,1)}, u32[]{:S(2)}, u32[]{:S(2)}) collective-permute-start(bf16[256,1024]{1,0:T(8,128)(2,1)S(1)} %get-tuple-element.211), channel_id=1, source_target_pairs={{7,5},{6,4},{5,3},{4,2},{3,1},{2,0},{15,13},{14,12},{13,11},{12,10... | collective-permute-start | bytes 1572872 | tf_op jit(solution)/shard_map/ppermute | solution.py:450
  611.7 28.6 %collective-permute-start.20 = (bf16[256,1024]{1,0:T(8,128)(2,1)S(1)}, bf16[256,1024]{1,0:T(8,128)(2,1)}, u32[]{:S(2)}, u32[]{:S(2)}) collective-permute-start(bf16[256,1024]{1,0:T(8,128)(2,1)S(1)} %get-tuple-element.207), channel_id=1, source_target_pairs={{7,5},{6,4},{5,3},{4,2},{3,1},{2,0},{15,13},{14,12},{13,11},{12,10... | collective-permute-start | bytes 1572872 | tf_op jit(solution)/shard_map/ppermute | solution.py:450
  613.0 16.1 %collective-permute-start.23 = (bf16[256,1024]{1,0:T(8,128)(2,1)S(1)}, bf16[256,1024]{1,0:T(8,128)(2,1)S(1)}, u32[]{:S(2)}, u32[]{:S(2)}) collective-permute-start(bf16[256,1024]{1,0:T(8,128)(2,1)S(1)} %get-tuple-element.204), channel_id=1, source_target_pairs={{0,2},{1,3},{2,4},{3,5},{8,10},{9,11},{10,12},{11,13},{16,18},{17,... | collective-permute-start | bytes 1572872 | tf_op jit(solution)/shard_map/ppermute | solution.py:449
  618.7 27.0 %collective-permute-start.27 = (bf16[256,1024]{1,0:T(8,128)(2,1)S(1)}, bf16[256,1024]{1,0:T(8,128)(2,1)}, u32[]{:S(2)}, u32[]{:S(2)}) collective-permute-start(bf16[256,1024]{1,0:T(8,128)(2,1)S(1)} %get-tuple-element.203), channel_id=1, source_target_pairs={{7,5},{6,4},{5,3},{4,2},{3,1},{2,0},{15,13},{14,12},{13,11},{12,10... | collective-permute-start | bytes 1572872 | tf_op jit(solution)/shard_map/ppermute | solution.py:450
  629.1 34.6 %collective-permute-start.30 = (bf16[128,2048]{1,0:T(8,128)(2,1)}, bf16[128,2048]{1,0:T(8,128)(2,1)}, u32[]{:S(2)}, u32[]{:S(2)}) collective-permute-start(bf16[128,2048]{1,0:T(8,128)(2,1)} %get-tuple-element.200), channel_id=1, source_target_pairs={{0,2},{1,3},{2,4},{3,5},{8,10},{9,11},{10,12},{11,13},{16,18},{17,... | collective-permute-start | bytes 1572872 | tf_op jit(solution)/shard_map/ppermute | solution.py:449
  635.4 87.0 %collective-permute-start.37 = (bf16[256,2048]{1,0:T(8,128)(2,1)}, bf16[256,2048]{1,0:T(8,128)(2,1)}, u32[]{:S(2)}, u32[]{:S(2)}) collective-permute-start(bf16[256,2048]{1,0:T(8,128)(2,1)} %get-tuple-element.195), channel_id=1, source_target_pairs={{0,2},{1,3},{2,4},{3,5},{4,6},{5,7},{8,10},{9,11},{10,12},{11,13},... | collective-permute-start | bytes 3145736 | tf_op jit(solution)/shard_map/ppermute | solution.py:449
  639.0 84.0 %collective-permute-start.40 = (bf16[256,2048]{1,0:T(8,128)(2,1)}, bf16[256,2048]{1,0:T(8,128)(2,1)}, u32[]{:S(2)}, u32[]{:S(2)}) collective-permute-start(bf16[256,2048]{1,0:T(8,128)(2,1)} %fusion.1), channel_id=1, source_target_pairs={{7,5},{6,4},{5,3},{4,2},{3,1},{2,0},{15,13},{14,12},{13,11},{12,10... | collective-permute-start | bytes 3145736 | tf_op jit(solution)/shard_map/ppermute | solution.py:450
  640.3 39.7 %collective-permute-start.17 = (bf16[256,1024]{1,0:T(8,128)(2,1)}, bf16[256,1024]{1,0:T(8,128)(2,1)}, u32[]{:S(2)}, u32[]{:S(2)}) collective-permute-start(bf16[256,1024]{1,0:T(8,128)(2,1)} %fusion.17), channel_id=1, source_target_pairs={{0,2},{1,3},{2,4},{3,5},{4,6},{5,7},{8,10},{9,11},{10,12},{11,13},... | collective-permute-start | bytes 1572872 | tf_op jit(solution)/shard_map/ppermute | solution.py:449
  645.6 45.6 %collective-permute-start.24 = (bf16[256,1024]{1,0:T(8,128)(2,1)}, bf16[256,1024]{1,0:T(8,128)(2,1)}, u32[]{:S(2)}, u32[]{:S(2)}) collective-permute-start(bf16[256,1024]{1,0:T(8,128)(2,1)} %fusion.13), channel_id=1, source_target_pairs={{0,2},{1,3},{2,4},{3,5},{4,6},{5,7},{8,10},{9,11},{10,12},{11,13},... | collective-permute-start | bytes 1572872 | tf_op jit(solution)/shard_map/ppermute | solution.py:449
  663.7 42.8 %collective-permute-start.10 = (bf16[256,1024]{1,0:T(8,128)(2,1)}, bf16[256,1024]{1,0:T(8,128)(2,1)S(1)}, u32[]{:S(2)}, u32[]{:S(2)}) collective-permute-start(bf16[256,1024]{1,0:T(8,128)(2,1)} %fusion.21), channel_id=1, source_target_pairs={{0,2},{1,3},{2,4},{3,5},{4,6},{5,7},{8,10},{9,11},{10,12},{11,13},... | collective-permute-start | bytes 1572872 | tf_op jit(solution)/shard_map/ppermute | solution.py:449
  680.0 32.7 %collective-permute-start.6 = (bf16[256,512]{1,0:T(8,128)(2,1)}, bf16[256,512]{1,0:T(8,128)(2,1)S(1)}, u32[]{:S(2)}, u32[]{:S(2)}) collective-permute-start(bf16[256,512]{1,0:T(8,128)(2,1)} %get-tuple-element.215), channel_id=1, source_target_pairs={{7,5},{6,4},{5,3},{4,2},{3,1},{2,0},{15,13},{14,12},{13,11},{12,10... | collective-permute-start | bytes 786440 | tf_op jit(solution)/shard_map/ppermute | solution.py:450
  691.2 26.1 %collective-permute-start.3 = (bf16[256,512]{1,0:T(8,128)(2,1)}, bf16[256,512]{1,0:T(8,128)(2,1)S(1)}, u32[]{:S(2)}, u32[]{:S(2)}) collective-permute-start(bf16[256,512]{1,0:T(8,128)(2,1)} %fusion.25), channel_id=1, source_target_pairs={{0,2},{1,3},{2,4},{3,5},{4,6},{5,7},{8,10},{9,11},{10,12},{11,13},... | collective-permute-start | bytes 786440 | tf_op jit(solution)/shard_map/ppermute | solution.py:449
  706.6 39.4 %collective-permute-start.34 = (bf16[128,2048]{1,0:T(8,128)(2,1)}, bf16[128,2048]{1,0:T(8,128)(2,1)S(1)}, u32[]{:S(2)}, u32[]{:S(2)}) collective-permute-start(bf16[128,2048]{1,0:T(8,128)(2,1)} %get-tuple-element.199), channel_id=1, source_target_pairs={{7,5},{6,4},{5,3},{4,2},{3,1},{2,0},{15,13},{14,12},{13,11},{12,10... | collective-permute-start | bytes 1572872 | tf_op jit(solution)/shard_map/ppermute | solution.py:450
  712.8 34.6 %collective-permute-start.31 = (bf16[128,2048]{1,0:T(8,128)(2,1)S(1)}, bf16[128,2048]{1,0:T(8,128)(2,1)S(1)}, u32[]{:S(2)}, u32[]{:S(2)}) collective-permute-start(bf16[128,2048]{1,0:T(8,128)(2,1)S(1)} %fusion.9), channel_id=1, source_target_pairs={{0,2},{1,3},{2,4},{3,5},{4,6},{5,7},{8,10},{9,11},{10,12},{11,13},... | collective-permute-start | bytes 1572872 | tf_op jit(solution)/shard_map/ppermute | solution.py:449
  722.4 4.6 collective-permute-start.42
  722.4 4.6 collective-permute-start.45
  725.5 14.0 %collective-permute-start.41 = (bf16[128,2048]{1,0:T(8,128)(2,1)S(1)}, bf16[128,2048]{1,0:T(8,128)(2,1)S(1)}, u32[]{:S(2)}, u32[]{:S(2)}) collective-permute-start(bf16[128,2048]{1,0:T(8,128)(2,1)S(1)} %dynamic-slice_bitcast_fusion.2), channel_id=1, source_target_pairs={{0,1},{1,0},{2,3},{3,2},{4,5},{5,4},{6,7},{7,6},{8,9},{9,8},{10,11... | collective-permute-start | bytes 1572872 | tf_op jit(solution)/shard_map/ppermute | solution.py:825
  726.9 1.5 collective-permute-start.48
  727.0 1.8 collective-permute-start.51
  728.5 25.7 %collective-permute-start.46 = (bf16[128,1024]{1,0:T(8,128)(2,1)S(1)}, bf16[128,1024]{1,0:T(8,128)(2,1)}, u32[]{:S(2)}, u32[]{:S(2)}) collective-permute-start(bf16[128,1024]{1,0:T(8,128)(2,1)S(1)} %add_convert_fusion.9), channel_id=1, source_target_pairs={{0,16},{8,24},{16,0},{24,8},{1,17},{9,25},{17,1},{25,9},{2,18},{10... | collective-permute-start | bytes 786440 | tf_op jit(solution)/shard_map/ppermute | solution.py:586
  728.9 26.9 %collective-permute-start.49 = (bf16[128,1024]{1,0:T(8,128)(2,1)S(1)}, bf16[128,1024]{1,0:T(8,128)(2,1)}, u32[]{:S(2)}, u32[]{:S(2)}) collective-permute-start(bf16[128,1024]{1,0:T(8,128)(2,1)S(1)} %add_convert_fusion.7), channel_id=1, source_target_pairs={{0,16},{8,24},{16,0},{24,8},{1,17},{9,25},{17,1},{25,9},{2,18},{10... | collective-permute-start | bytes 786440 | tf_op jit(solution)/shard_map/ppermute | solution.py:586
  739.5 34.9 %collective-permute-start.43 = (bf16[128,512]{1,0:T(8,128)(2,1)S(1)}, bf16[128,512]{1,0:T(8,128)(2,1)}, u32[]{:S(2)}, u32[]{:S(2)}) collective-permute-start(bf16[128,512]{1,0:T(8,128)(2,1)S(1)} %add_convert_fusion.11), channel_id=1, source_target_pairs={{0,16},{8,24},{16,0},{24,8},{1,17},{9,25},{17,1},{25,9},{2,18},{10... | collective-permute-start | bytes 393224 | tf_op jit(solution)/shard_map/ppermute | solution.py:586
  746.0 10.9 %collective-permute-start.52 = (bf16[128,1024]{1,0:T(8,128)(2,1)S(1)}, bf16[128,1024]{1,0:T(8,128)(2,1)S(1)}, u32[]{:S(2)}, u32[]{:S(2)}) collective-permute-start(bf16[128,1024]{1,0:T(8,128)(2,1)S(1)} %add_convert_fusion.5), channel_id=1, source_target_pairs={{0,16},{8,24},{16,0},{24,8},{1,17},{9,25},{17,1},{25,9},{2,18},{10... | collective-permute-start | bytes 786440 | tf_op jit(solution)/shard_map/ppermute | solution.py:586
  754.1 3.4 collective-permute-start.54
  754.2 3.5 collective-permute-start.57
  755.7 29.8 %collective-permute-start.47 = (bf16[128,1024]{1,0:T(8,128)(2,1)S(1)}, bf16[128,1024]{1,0:T(8,128)(2,1)S(1)}, u32[]{:S(2)}, u32[]{:S(2)}) collective-permute-start(bf16[128,1024]{1,0:T(8,128)(2,1)S(1)} %add_convert_fusion.8.keep_ref), channel_id=1, source_target_pairs={{0,8},{8,0},{16,24},{24,16},{1,9},{9,1},{17,25},{25,17},{2,10},{10... | collective-permute-start | bytes 786440 | tf_op jit(solution)/shard_map/ppermute | solution.py:587
  756.9 23.8 %collective-permute-start.50 = (bf16[128,1024]{1,0:T(8,128)(2,1)S(1)}, bf16[128,1024]{1,0:T(8,128)(2,1)S(1)}, u32[]{:S(2)}, u32[]{:S(2)}) collective-permute-start(bf16[128,1024]{1,0:T(8,128)(2,1)S(1)} %add_convert_fusion.6.keep_ref), channel_id=1, source_target_pairs={{0,8},{8,0},{16,24},{24,16},{1,9},{9,1},{17,25},{25,17},{2,10},{10... | collective-permute-start | bytes 786440 | tf_op jit(solution)/shard_map/ppermute | solution.py:587
  757.5 18.4 %collective-permute-start.53 = (bf16[128,1024]{1,0:T(8,128)(2,1)S(1)}, bf16[128,1024]{1,0:T(8,128)(2,1)S(1)}, u32[]{:S(2)}, u32[]{:S(2)}) collective-permute-start(bf16[128,1024]{1,0:T(8,128)(2,1)S(1)} %add_convert_fusion.4.keep_ref), channel_id=1, source_target_pairs={{0,8},{8,0},{16,24},{24,16},{1,9},{9,1},{17,25},{25,17},{2,10},{10... | collective-permute-start | bytes 786440 | tf_op jit(solution)/shard_map/ppermute | solution.py:587
  757.8 8.7 %collective-permute-start.55 = (bf16[64,2048]{1,0:T(8,128)(2,1)S(1)}, bf16[64,2048]{1,0:T(8,128)(2,1)S(1)}, u32[]{:S(2)}, u32[]{:S(2)}) collective-permute-start(bf16[64,2048]{1,0:T(8,128)(2,1)S(1)} %add_convert_fusion.3), channel_id=1, source_target_pairs={{0,16},{8,24},{16,0},{24,8},{1,17},{9,25},{17,1},{25,9},{2,18},{10... | collective-permute-start | bytes 786440 | tf_op jit(solution)/shard_map/ppermute | solution.py:586
  766.5 7.9 collective-permute-start.58
  774.3 25.6 %collective-permute-start.56 = (bf16[64,2048]{1,0:T(8,128)(2,1)S(1)}, bf16[64,2048]{1,0:T(8,128)(2,1)S(1)}, u32[]{:S(2)}, u32[]{:S(2)}) collective-permute-start(bf16[64,2048]{1,0:T(8,128)(2,1)S(1)} %add_convert_fusion.2.keep_ref), channel_id=1, source_target_pairs={{0,8},{8,0},{16,24},{24,16},{1,9},{9,1},{17,25},{25,17},{2,10},{10... | collective-permute-start | bytes 786440 | tf_op jit(solution)/shard_map/ppermute | solution.py:587
  774.4 19.9 %collective-permute-start.59 = (bf16[64,2048]{1,0:T(8,128)(2,1)S(1)}, bf16[64,2048]{1,0:T(8,128)(2,1)S(1)}, u32[]{:S(2)}, u32[]{:S(2)}) collective-permute-start(bf16[64,2048]{1,0:T(8,128)(2,1)S(1)} %add_convert_fusion.keep_ref), channel_id=1, source_target_pairs={{0,8},{8,0},{16,24},{24,16},{1,9},{9,1},{17,25},{25,17},{2,10},{10... | collective-permute-start | bytes 786440 | tf_op jit(solution)/shard_map/ppermute | solution.py:587
  776.0 14.3 %collective-permute-start.44 = (bf16[128,512]{1,0:T(8,128)(2,1)S(1)}, bf16[128,512]{1,0:T(8,128)(2,1)S(1)}, u32[]{:S(2)}, u32[]{:S(2)}) collective-permute-start(bf16[128,512]{1,0:T(8,128)(2,1)S(1)} %add_convert_fusion.10.keep_ref), channel_id=1, source_target_pairs={{0,8},{8,0},{16,24},{24,16},{1,9},{9,1},{17,25},{25,17},{2,10},{10... | collective-permute-start | bytes 393224 | tf_op jit(solution)/shard_map/ppermute | solution.py:587
  (46 other events, 562.3 us)
Sparse Core Ops, SparseCore 0:
  373.6 63.3 reduce-scatter.3

commit v2 on v1

--- a/solution.py
+++ b/solution.py
@@ -149,20 +149,14 @@
     )(lengths, packed, packed, packed)
 
 
-def attn_back_kernel(len_ref, q_ref, k_ref, v_ref, d_ref, o_ref, lse_ref, dq_ref, dk_ref, dv_ref, dk_acc, dv_acc):
-    i = pl.program_id(1)
-    count = key_blocks(len_ref, i)
+def attention_back_step(len_ref, i, q_ref, k_ref, v_ref, d_ref, o_ref, lse_ref, dq_ref, dk_acc, dv_acc, count=None):
+    if count is None:
+        count = jnp.minimum(i + 1, max_blocks())
     row = i * BQ + lax.broadcasted_iota(jnp.int32, (1, BQ), 1)
     start = doc_start(len_ref, row)
     lane = lax.broadcasted_iota(jnp.int32, (BQ, 128), 1)
     group = H // KVH
     scale = jnp.asarray(HD**-0.5, bf16)
-
-    @pl.when(i == 0)
-    def _():
-        dk_acc[...] = jnp.zeros_like(dk_acc)
-        dv_acc[...] = jnp.zeros_like(dv_acc)
-
     tile = jnp.zeros((BQ, 128), f32)
     for h in range(2 * group):
         cols = slice(h * HD, (h + 1) * HD)
@@ -206,6 +200,19 @@
             dk_acc[pl.ds(base, span), :] += jnp.concatenate(dks, axis=1)
             dv_acc[pl.ds(base, span), :] += jnp.concatenate(dvs, axis=1)
 
+
+def attn_back_kernel(len_ref, q_ref, k_ref, v_ref, d_ref, o_ref, lse_ref, dq_ref, dk_ref, dv_ref, dk_acc, dv_acc):
+    i = pl.program_id(1)
+
+    @pl.when(i == 0)
+    def _():
+        dk_acc[...] = jnp.zeros_like(dk_acc)
+        dv_acc[...] = jnp.zeros_like(dv_acc)
+
+    attention_back_step(
+        len_ref, i, q_ref, k_ref, v_ref, d_ref, o_ref, lse_ref, dq_ref, dk_acc, dv_acc, key_blocks(len_ref, i)
+    )
+
     @pl.when(i == pl.num_programs(1) - 1)
     def _():
         dk_ref[...] = dk_acc[...].astype(bf16)
@@ -255,13 +262,15 @@
 
 
 def ffn_kernel(table_ref, x_ref, mixed_ref, t_ref, ids_ref, g_ref, proj_ref, wf_ref, down_ref,
-               middle_ref, second_ref, hidden_ref, dboth_ref, dy_ref):
+               middle_ref, second_ref, hidden_ref, dboth_ref, dy_ref, c_ref):
     middle = x_ref[...].astype(f32) + mm(mixed_ref[...], proj_ref[...])
     middle_ref[...] = middle
     r = lax.rsqrt(jnp.mean(middle * middle, axis=-1, keepdims=True) + norm_eps)
     second = (middle * r * g_ref[1:2, :]).astype(bf16)
     second_ref[...] = second
-    dy = (token_weight(table_ref, ids_ref[...]) * t_ref[...].astype(f32)).astype(bf16)
+    c = token_weight(table_ref, ids_ref[...])
+    c_ref[...] = jnp.broadcast_to(c, c_ref.shape)
+    dy = (c * t_ref[...].astype(f32)).astype(bf16)
     dy_ref[...] = dy
     step = 512
     for c in range(0, FF, step):
@@ -285,7 +294,7 @@
             num_scalar_prefetch=1,
             grid=(LEN // BQ,),
             in_specs=[rowb(width), rowb(H * HD), rowb(width), rowb(1), whole(gains), whole(proj), whole(wf), whole(down)],
-            out_specs=[rowb(width), rowb(width), rowb(FF), rowb(2 * FF), rowb(width)],
+            out_specs=[rowb(width), rowb(width), rowb(FF), rowb(2 * FF), rowb(width), rowb(128)],
         ),
         out_shape=[
             jax.ShapeDtypeStruct((LEN, width), f32),
@@ -293,6 +302,7 @@
             jax.ShapeDtypeStruct((LEN, FF), bf16),
             jax.ShapeDtypeStruct((LEN, 2 * FF), bf16),
             jax.ShapeDtypeStruct((LEN, width), bf16),
+            jax.ShapeDtypeStruct((LEN, 128), f32),
         ],
         compiler_params=params(),
         cost_estimate=pl.CostEstimate(flops=2 * LEN * width * FF * 4, bytes_accessed=40 << 20, transcendentals=0),
@@ -434,23 +444,6 @@
     return (a.astype(f32) + b.astype(f32)).astype(a.dtype)
 
 
-def line_sum(blocks, z, line):
-    right = left = None
-    for step in range(1, line):
-        at_right = jnp.clip(line - step + z, 0, line - 1)
-        at_left = jnp.clip(z - line + step, 0, line - 1)
-        to_right = lax.dynamic_index_in_dim(blocks, at_right, 0, keepdims=False)
-        to_left = lax.dynamic_index_in_dim(blocks, at_left, 0, keepdims=False)
-        if right is not None:
-            to_right = add_low(to_right, right)
-            to_left = add_low(to_left, left)
-        pairs = [(k * 2 + y, k * 2 + 2 + y) for k in range(step) for y in range(2)]
-        last = 2 * line - 1
-        right = lax.ppermute(to_right, "fsdp", pairs)
-        left = lax.ppermute(to_left, "fsdp", [(last - a, last - b) for a, b in pairs])
-    return right, left
-
-
 beta_first = 0.9
 beta_second = 0.95
 adam_eps = 1e-08
@@ -476,12 +469,13 @@
 
 def adam_kernel(place_ref, own_ref, *refs, terms, rate):
     refs = list(refs)
-    more = [refs.pop(0) for _ in range(terms)]
+    slots = refs.pop(0) if terms else None
     first_ref, second_ref, w_ref = refs[:3]
     grad_ref, first_new_ref, second_new_ref, keep_ref, send_ref = refs[-5:]
     grad = own_ref[0].astype(f32)
-    for term in more:
-        grad = grad + term[...].astype(f32)
+    if terms:
+        grad = grad + slots[0].astype(f32)
+        grad = grad + jnp.where(place_ref[3] == 1, slots[1].astype(f32), 0.0)
     first_new, second_new, delta = adam_step(grad, first_ref[...], second_ref[...], w_ref[...], rate)
     grad_ref[...] = grad
     first_new_ref[...] = first_new
@@ -503,7 +497,7 @@
 
 def adam_piece(place, own, terms, first, second, w, held, rows, row_at, col_at, cols, tile, rate):
     at = lambda j, p: (row_at // rows, col_at // tile + j)
-    piece = pl.BlockSpec((rows, tile), lambda j, p: (0, j))
+    piece = pl.BlockSpec((pl.Element(2), pl.Element(rows), pl.Element(tile)), lambda j, p: (2, 0, j * tile))
     half = pl.BlockSpec((rows // 2, tile), lambda j, p: (0, j))
     state = pl.BlockSpec((rows, tile), at)
     full = jax.ShapeDtypeStruct(first.shape, f32)
@@ -758,6 +752,300 @@
     return [gain_full] + [a.reshape(-1, a.shape[-1]) for a in full[1:]]
 
 
+PIECES = ("down", "gate", "up", "proj", "q", "kv")
+
+
+def back_kernel(*refs, names, line):
+    R = dict(zip(names, refs))
+    r, f = lax.axis_index("rep"), lax.axis_index("fsdp")
+    z, y = f // 2, f % 2
+    n = 2 * line
+    barrier = pltpu.get_barrier_semaphore()
+    for step in range(1, n):
+        pl.semaphore_signal(barrier, inc=1, device_id=(r, lax.rem(f + step, n)), device_id_type=pl.DeviceIdType.MESH)
+    pl.semaphore_wait(barrier, n - 1)
+
+    loads = ("proj", "wf", "down", "wq")
+    load = lambda k: pltpu.make_async_copy(R[loads[k]], R["v_" + loads[k]], R["load_sem"].at[k])
+    for k in range(len(loads)):
+        load(k).start()
+
+    def remote(src, dst, send, recv, to):
+        return pltpu.make_async_remote_copy(
+            src_ref=src, dst_ref=dst, send_sem=send, recv_sem=recv, device_id=(r, to), device_id_type=pl.DeviceIdType.MESH
+        )
+
+    def run(body, grid, ins, outs):
+        pltpu.emit_pipeline(body, grid=grid, in_specs=[s for _, s in ins], out_specs=[s for _, s in outs])(
+            *[a for a, _ in ins], *[a for a, _ in outs]
+        )
+
+    rows_of = {p: R["own_" + p].shape[1] for p in PIECES}
+    cols_of = {p: R["own_" + p].shape[2] for p in PIECES}
+    sources = {
+        "down": ("hidden", [("dy", 0, R["dy"].shape[1])]),
+        "gate": ("second", [("dboth", 0, FF)]),
+        "up": ("second", [("dboth", 1, FF)]),
+        "proj": ("mixed", [("dlow", 0, R["dlow"].shape[1])]),
+        "q": ("first", [("dq", 0, H * HD)]),
+        "kv": ("first", [("dk", 0, KVH * HD), ("dv", 0, KVH * HD)]),
+    }
+
+    def gradient(p, side, out, add=None):
+        a, bs = sources[p]
+        rows, cols = rows_of[p], cols_of[p]
+        block = pl.BlockSpec((1, rows, cols), lambda j: (j, 0, 0))
+        ins = [(R[a], pl.BlockSpec((LEN, rows), lambda j: (0, j * 2 + side)))]
+        for b, at, width in bs:
+            ins.append((R[b], pl.BlockSpec((LEN, width), functools.partial(lambda at, j: (0, at), at))))
+        if add is not None:
+            ins.append((add, block))
+
+        def step(*refs):
+            out_ref, a_ref, b_refs = refs[-1], refs[0], refs[1 : 1 + len(bs)]
+            col = 0
+            for b_ref in b_refs:
+                width = b_ref.shape[1]
+                g = mm(a_ref[...], b_ref[...], TN)
+                if add is not None:
+                    g = g + refs[-2][0, :, col : col + width].astype(f32)
+                out_ref[0, :, col : col + width] = g.astype(bf16)
+                col += width
+
+        run(step, (line,), ins, [(out, block)])
+
+    def pair_copy(p):
+        k = PIECES.index(p)
+        return remote(R["away_" + p], R["came_" + p], R["y_send"].at[k], R["y_recv"].at[k], f + 1 - 2 * y)
+
+    def send_away(p):
+        gradient(p, 1 - y, R["away_" + p])
+        pair_copy(p).start()
+
+    middle = (z > 0) & (z < line - 1)
+    low = z < line // 2
+    inner = jnp.where(low, f + 2, f - 2)
+    outer = jnp.where(low, f - 2, f + 2)
+
+    def end_copy(p, k):
+        i = PIECES.index(p)
+        t = jnp.where(low, line - 1 - k, k)
+        return remote(R["own_" + p].at[t], R["slot_" + p].at[k], R["z_send"].at[i, k], R["z_recv"].at[i, k], inner)
+
+    def middle_copy(p, k):
+        i = PIECES.index(p)
+        slot = (4, 3, 2)[k]
+        to = outer if k == 2 else inner
+        return remote(R["msg_" + p].at[k], R["slot_" + p].at[slot], R["z_send"].at[i, k], R["z_recv"].at[i, slot], to)
+
+    def slot_wait(p, slot):
+        i = PIECES.index(p)
+        ref = R["slot_" + p].at[slot]
+        remote(ref, ref, R["z_send"].at[i, 0], R["z_recv"].at[i, slot], inner).wait_recv()
+
+    def keep(p):
+        pair_copy(p).wait_recv()
+        gradient(p, y, R["own_" + p], R["came_" + p])
+
+        @pl.when(~middle)
+        def _():
+            for k in range(3):
+                end_copy(p, k).start()
+
+    def serve(p, k):
+        @pl.when(middle)
+        def _():
+            slot = (0, 1, 4)[k]
+            slot_wait(p, slot)
+            t = (3 * (2 - z), 3 - z, 3 * (z - 1))[k]
+            rows, cols = rows_of[p], cols_of[p]
+            block = pl.BlockSpec((rows // 2, cols), lambda j: (j, 0))
+
+            def step(a_ref, b_ref, o_ref):
+                o_ref[...] = (a_ref[...].astype(f32) + b_ref[...].astype(f32)).astype(bf16)
+
+            run(step, (2,), [(R["own_" + p].at[t], block), (R["slot_" + p].at[slot], block)], [(R["msg_" + p].at[k], block)])
+            middle_copy(p, k).start()
+
+    rowb = lambda width: pl.BlockSpec((BQ, width), lambda i: (i, 0))
+    width = R["x"].shape[1]
+    R["gain_acc"][...] = jnp.zeros_like(R["gain_acc"])
+    gain_rows = R["gain"][...]
+
+    def mid_step(middle_ref, hidden_ref, dboth_ref, t_ref, c_ref, act_ref, dmid_ref, dlow_ref, dmix_ref):
+        mid_v = middle_ref[...]
+        act_ref[...] = (mid_v + mm(hidden_ref[...], R["v_down"][...])).astype(bf16)
+        inv = lax.rsqrt(jnp.mean(mid_v * mid_v, axis=-1, keepdims=True) + norm_eps)
+        n2 = mid_v * inv
+        ds2 = mm(dboth_ref[...], R["v_wf"][...], NT)
+        prod = ds2 * n2
+        R["gain_acc"][8:16, :] += jnp.sum(prod.reshape(BQ // 8, 8, width), axis=0)
+        g = gain_rows[1:2, :]
+        dy = c_ref[:, 0:1] * t_ref[...].astype(f32)
+        dmid = dy + inv * (ds2 * g - n2 * jnp.mean(prod * g, axis=-1, keepdims=True))
+        dmid_ref[...] = dmid
+        dlow = dmid.astype(bf16)
+        dlow_ref[...] = dlow
+        dmix_ref[...] = mm(dlow, R["v_proj"][...], NT).astype(bf16)
+
+    def mid_phase():
+        run(
+            mid_step,
+            (LEN // BQ,),
+            [(R["middle"], rowb(width)), (R["hidden"], rowb(FF)), (R["dboth"], rowb(2 * FF)), (R["target"], rowb(width)), (R["c"], rowb(128))],
+            [(R["act"], rowb(width)), (R["dmid"], rowb(width)), (R["dlow"], rowb(width)), (R["dmix"], rowb(H * HD))],
+        )
+
+    qw = H // 2 * HD
+    kcol = H * HD // 128
+    vcol = kcol + KVH * HD // 128
+
+    def attention_phase(p):
+        qspec = pl.BlockSpec((BQ, qw), lambda i: (i, p))
+        whole = lambda at: pl.BlockSpec((LEN, 128), lambda i: (0, at))
+        R["dk_acc"][...] = jnp.zeros_like(R["dk_acc"])
+        R["dv_acc"][...] = jnp.zeros_like(R["dv_acc"])
+
+        def step(q_ref, k_ref, v_ref, d_ref, o_ref, lse_ref, dq_ref):
+            attention_back_step(R["lengths"], pl.program_id(0), q_ref, k_ref, v_ref, d_ref, o_ref, lse_ref, dq_ref, R["dk_acc"], R["dv_acc"])
+
+        pltpu.emit_pipeline(
+            step, grid=(LEN // BQ,),
+            in_specs=[qspec, whole(kcol + p), whole(vcol + p), qspec, qspec, pl.BlockSpec((8, BQ), lambda i: (p, i))],
+            out_specs=[qspec],
+        )(R["packed"], R["packed"], R["packed"], R["dmix"], R["mixed"], R["lse"], R["dq"])
+
+        def flush(dk_ref, dv_ref):
+            dk_ref[...] = R["dk_acc"][...].astype(bf16)
+            dv_ref[...] = R["dv_acc"][...].astype(bf16)
+
+        run(flush, (1,), [], [(R["dk"], pl.BlockSpec((LEN, 128), lambda i: (0, p))), (R["dv"], pl.BlockSpec((LEN, 128), lambda i: (0, p)))])
+
+    def input_step(x_ref, dmid_ref, dq_ref, dk_ref, dv_ref, out_ref):
+        x = x_ref[...].astype(f32)
+        inv = lax.rsqrt(jnp.mean(x * x, axis=-1, keepdims=True) + norm_eps)
+        n1 = x * inv
+        q, k = H * HD, H * HD + KVH * HD
+        w = R["v_wq"]
+        ds1 = mm(dq_ref[...], w[:, :q], NT) + mm(dk_ref[...], w[:, q:k], NT) + mm(dv_ref[...], w[:, k:], NT)
+        prod = ds1 * n1
+        R["gain_acc"][0:8, :] += jnp.sum(prod.reshape(BQ // 8, 8, width), axis=0)
+        g = gain_rows[0:1, :]
+        out_ref[...] = (dmid_ref[...] + inv * (ds1 * g - n1 * jnp.mean(prod * g, axis=-1, keepdims=True))).astype(bf16)
+
+    def input_phase():
+        run(
+            input_step,
+            (LEN // BQ,),
+            [(R["x"], rowb(width)), (R["dmid"], rowb(width)), (R["dq"], rowb(H * HD)), (R["dk"], rowb(KVH * HD)), (R["dv"], rowb(KVH * HD))],
+            [(R["xgrad"], rowb(width))],
+        )
+
+    part = width // n
+
+    def gain_copy(step, receive=False):
+        peer = lax.rem(f + step, n)
+        home = lax.rem(f + n - step, n) if receive else f
+        return remote(
+            R["gain_acc"].at[:, pl.ds(pl.multiple_of(peer * part, part), part)], R["gain_got"].at[home],
+            R["g_send"].at[step - 1], R["g_recv"].at[step - 1], peer,
+        )
+
+    own_gain = pltpu.make_async_copy(
+        R["gain_acc"].at[:, pl.ds(pl.multiple_of(f * part, part), part)], R["gain_got"].at[f], R["g_send"].at[n - 1]
+    )
+
+    for p in ("down", "gate", "up"):
+        send_away(p)
+    for k in range(3):
+        load(k).wait()
+    mid_phase()
+    send_away("proj")
+    keep("down")
+    attention_phase(0)
+    serve("down", 0)
+    attention_phase(1)
+    serve("down", 1)
+    keep("gate")
+    serve("down", 2)
+    send_away("q")
+    send_away("kv")
+    serve("gate", 0)
+    load(3).wait()
+    input_phase()
+    for step in range(1, n):
+        gain_copy(step).start()
+    own_gain.start()
+    serve("gate", 1)
+    keep("up")
+    serve("gate", 2)
+    for k in range(3):
+        serve("up", k)
+    for p in ("proj", "q", "kv"):
+        keep(p)
+        for k in range(3):
+            serve(p, k)
+
+    for step in range(1, n):
+        gain_copy(step, True).wait_recv()
+        gain_copy(step).wait_send()
+    own_gain.wait()
+    for p in PIECES:
+        pair_copy(p).wait_send()
+        slot_wait(p, 2)
+
+        @pl.when(middle)
+        def _():
+            slot_wait(p, 3)
+            for k in range(3):
+                middle_copy(p, k).wait_send()
+
+        @pl.when(~middle)
+        def _():
+            for k in range(3):
+                end_copy(p, k).wait_send()
+
+
+def backward(lengths, gain, arrays, n, rows_in, rows_out):
+    line = n // 2
+    width = arrays["x"].shape[1]
+    kvw = KVH * HD
+    sizes = {
+        "down": (rows_out, width), "gate": (rows_in, FF), "up": (rows_in, FF),
+        "proj": (rows_out, width), "q": (rows_in, H * HD), "kv": (rows_in, 2 * kvw),
+    }
+    outs = {
+        "act": ((LEN, width), bf16), "dmid": ((LEN, width), f32), "dlow": ((LEN, width), bf16),
+        "dmix": ((LEN, H * HD), bf16), "dq": ((LEN, H * HD), bf16), "dk": ((LEN, kvw), bf16), "dv": ((LEN, kvw), bf16),
+        "xgrad": ((LEN, width), bf16), "gain_got": ((n, 16, width // n), f32),
+    }
+    for p, (rows, cols) in sizes.items():
+        for kind, count in (("away_", line), ("came_", line), ("own_", line), ("slot_", 5), ("msg_", 3)):
+            outs[kind + p] = ((count, rows, cols), bf16)
+    dma = pltpu.SemaphoreType.DMA
+    pieces = len(PIECES)
+    scratch = {
+        "v_proj": pltpu.VMEM(arrays["proj"].shape, bf16), "v_wf": pltpu.VMEM(arrays["wf"].shape, bf16),
+        "v_down": pltpu.VMEM(arrays["down"].shape, bf16), "v_wq": pltpu.VMEM(arrays["wq"].shape, bf16),
+        "gain_acc": pltpu.VMEM((16, width), f32), "dk_acc": pltpu.VMEM((LEN, 128), f32), "dv_acc": pltpu.VMEM((LEN, 128), f32),
+        "load_sem": dma((4,)), "y_send": dma((pieces,)), "y_recv": dma((pieces,)),
+        "z_send": dma((pieces, 3)), "z_recv": dma((pieces, 5)), "g_send": dma((n,)), "g_recv": dma((n,)),
+    }
+    names = ["lengths", "gain", *arrays, *outs, *scratch]
+    anywhere = pl.BlockSpec(memory_space=pl.ANY)
+    got = pl.pallas_call(
+        functools.partial(back_kernel, names=names, line=line),
+        in_specs=[pl.BlockSpec(memory_space=pltpu.SMEM), pl.BlockSpec(memory_space=pltpu.VMEM)] + [anywhere] * len(arrays),
+        out_specs=[anywhere] * len(outs),
+        out_shape=[jax.ShapeDtypeStruct(*v) for v in outs.values()],
+        scratch_shapes=list(scratch.values()),
+        compiler_params=pltpu.CompilerParams(collective_id=1, has_side_effects=True, vmem_limit_bytes=62 << 20),
+        cost_estimate=pl.CostEstimate(flops=200 << 30, bytes_accessed=400 << 20, transcendentals=0),
+        name="backward",
+    )(lengths, gain, *arrays.values())
+    return dict(zip(outs, got))
+
+
 rate_in = 0.02
 rate_out = 0.08
 rate_gains = 1.2
@@ -787,7 +1075,8 @@
     f, r = lax.axis_index("fsdp"), lax.axis_index("rep")
     z, y = f // 2, f % 2
     direct = by_neighbours(n, rep)
-    place = jnp.stack([z if direct else 0 * z, r % 2, y if direct else 0 * y]).astype(jnp.int32)
+    inside = (z > 0) & (z < line - 1)
+    place = jnp.stack([z if direct else 0 * z, r % 2, y, inside]).astype(jnp.int32)
     rows_in, rows_out = w_in.shape[0], w_out.shape[1]
     gain_full, wq, proj, wf, down = all_weights(w_in, w_out, gains, n, rep)
     x, tgt, lengths = tokens[0], target[0], doc_lengths[0]
@@ -795,49 +1084,42 @@
 
     first_low, packed = qkv(x, gain_full, wq)
     mixed, lse = attention(lengths, packed)
-    middle, second_low, hidden, d_both, dy = ffn(corpus_weights, x, mixed, tgt, ids, gain_full, proj, wf, down)
-
-    every = jnp.arange(line, dtype=jnp.int32)
-    ours, theirs = every * 2 + y, every * 2 + 1 - y
-    flip = flip_pairs(n)
-
-    def by_library(a, bs, name):
-        block = 2 * BQ if a.shape[1] % (2 * BQ) == 0 else BQ
-        every_row = jnp.arange(a.shape[1] // block, dtype=jnp.int32)
-        total = grad_rows(every_row, a, bs, block, name=name)
-        return lax.psum_scatter(total.reshape(a.shape[1], -1), "fsdp", scatter_dimension=0, tiled=True)[None], ()
-
-    def pair_first(a, bs, rows, name):
-        if not direct:
-            return by_library(a, bs, name)
-        away = grad_rows(theirs, a, bs, rows, name=name + "_send")
-        came = lax.ppermute(away, "fsdp", flip)
-        total = grad_rows(ours, a, bs, rows, add=came, name=name + "_keep")
-        return total, line_sum(total, z, line)
-
-    def line_first(a, bs, rows, name):
-        if not direct:
-            return by_library(a, bs, name)
-        total = grad_rows(every, a, bs, 2 * rows, name=name)
-        right, left = line_sum(total, z, line)
-        mine = lax.dynamic_index_in_dim(total, z, 0, keepdims=False)
-        mine = (mine.astype(f32) + right.astype(f32) + left.astype(f32)).astype(bf16).reshape(2, rows, -1)
-        came = lax.ppermute(lax.dynamic_index_in_dim(mine, 1 - y, 0, keepdims=False), "fsdp", flip)
-        return mine, (came,)
-
-    gate_sum = pair_first(second_low, [(d_both, 0, FF)], rows_in, "grad_gate")
-    down_sum = line_first(hidden, [(dy, 0, dy.shape[1])], rows_out, "grad_down")
-    up_sum = pair_first(second_low, [(d_both, 1, FF)], rows_in, "grad_up")
-    activations, d_mid, d_low, d_mix, gain_two = mid(
-        corpus_weights, middle, hidden, d_both, tgt, ids, gain_full, proj, wf, down
-    )
-    proj_sum = pair_first(mixed, [(d_low, 0, d_low.shape[1])], rows_out, "grad_proj")
-    dq, dk, dv = attention_back(lengths, packed, d_mix, mixed, lse)
-    q_sum = pair_first(first_low, [(dq, 0, H * HD)], rows_in, "grad_q")
-    kv_sum = pair_first(first_low, [(dk, 0, KVH * HD), (dv, 0, KVH * HD)], rows_in, "grad_kv")
-    input_grad, gain_one = input_back(x, d_mid, dq, dk, dv, gain_full, wq)
-
-    by_y = place.at[0].set(place[2])
+    middle, second_low, hidden, d_both, dy, c = ffn(corpus_weights, x, mixed, tgt, ids, gain_full, proj, wf, down)
+
+    if direct:
+        got = backward(
+            lengths, gain_full,
+            dict(x=x, target=tgt, c=c, middle=middle, hidden=hidden, second=second_low, dboth=d_both, dy=dy, mixed=mixed,
+                 packed=packed, lse=lse, first=first_low, proj=proj, wf=wf, down=down, wq=wq),
+            n, rows_in, rows_out,
+        )
+        activations, input_grad = got["act"], got["xgrad"]
+        gain_share = jnp.sum(got["gain_got"].reshape(n, 2, 8, -1), axis=(0, 2))
+        gate_sum, up_sum, q_sum, kv_sum, down_sum, proj_sum = (
+            (got["own_" + p], (got["slot_" + p],)) for p in ("gate", "up", "q", "kv", "down", "proj")
+        )
+    else:
+
+        def by_library(a, bs, name):
+            block = 2 * BQ if a.shape[1] % (2 * BQ) == 0 else BQ
+            every_row = jnp.arange(a.shape[1] // block, dtype=jnp.int32)
+            total = grad_rows(every_row, a, bs, block, name=name)
+            return lax.psum_scatter(total.reshape(a.shape[1], -1), "fsdp", scatter_dimension=0, tiled=True)[None], ()
+
+        gate_sum = by_library(second_low, [(d_both, 0, FF)], "grad_gate")
+        down_sum = by_library(hidden, [(dy, 0, dy.shape[1])], "grad_down")
+        up_sum = by_library(second_low, [(d_both, 1, FF)], "grad_up")
+        activations, d_mid, d_low, d_mix, gain_two = mid(
+            corpus_weights, middle, hidden, d_both, tgt, ids, gain_full, proj, wf, down
+        )
+        proj_sum = by_library(mixed, [(d_low, 0, d_low.shape[1])], "grad_proj")
+        dq, dk, dv = attention_back(lengths, packed, d_mix, mixed, lse)
+        q_sum = by_library(first_low, [(dq, 0, H * HD)], "grad_q")
+        kv_sum = by_library(first_low, [(dk, 0, KVH * HD), (dv, 0, KVH * HD)], "grad_kv")
+        input_grad, gain_one = input_back(x, d_mid, dq, dk, dv, gain_full, wq)
+        both = jnp.stack([jnp.sum(gain_one, axis=0), jnp.sum(gain_two, axis=0)])
+        gain_share = lax.psum_scatter(both, "fsdp", scatter_dimension=1, tiled=True)
+
     flat = lambda a: a.reshape(-1, a.shape[-1])
 
     def weight_steps(pieces, first, second, w, outer, rate):
@@ -859,7 +1141,7 @@
     ]
     width = w_out.shape[2]
     out_pieces = [
-        (by_y, (down_sum, rows_out, rows_out, 0, width, 512)),
+        (place, (down_sum, rows_out, rows_out, 0, width, 512)),
         (place, (proj_sum, rows_out, 0, 0, width, 512)),
     ]
     out_grads, out_steps = weight_steps(
@@ -867,8 +1149,6 @@
     )
     in_grads, in_steps = weight_steps(in_pieces, first_in[0], second_in[0], w_in, outer_in, rate_in)
 
-    gain_full = jnp.stack([jnp.sum(gain_one, axis=0), jnp.sum(gain_two, axis=0)])
-    gain_share = lax.psum_scatter(gain_full, "fsdp", scatter_dimension=1, tiled=True)
     first_gains_new, second_gains_new, delta = adam_step(gain_share, first_gains[0], second_gains[0], gains, rate_gains)
     sum_gains = lax.psum(delta, "rep")
     diff_gains, outer_gains_new, new_gains = outer_step(sum_gains, outer_gains, gains, rep)

time: 825 us -> 660 us (0.80)
  starting transfers between devices: 167 us -> 7.22 us
  Pallas kernels: 423 us -> 582 us
  waiting for transfers between devices: 134 us -> 28.2 us
  other arithmetic: 40.3 us -> 7.32 us
  between operations: 15.6 us -> 1.57 us
  local copies, waits for them, and re-layouts: 26.9 us -> 15.2 us
    ppermute x42 -> x0, starting transfers between devices: 159 us -> none  [the longest x18 125 us: line_sum(): right = lax.ppermute(to_right, 'fsdp', pairs)]
    pallas_call x14 -> x1, Pallas kernels: 158 us -> 317 us  [backward(): pl.pallas_call(functools.partial(back_kernel, names=names, line=line), in...]
    ppermute x42 -> x0, waiting for transfers between devices: 63.3 us -> none  [the longest x18 34.6 us: line_sum(): right = lax.ppermute(to_right, 'fsdp', pairs)]
    unnamed x2 -> x0, waiting for transfers between devices: 54.4 us -> none
    convert_element_type x30 -> x12, other arithmetic: 30.9 us -> 1.63 us  [add_low(): return (a.astype(f32) + b.astype(f32)).astype(a.dtype)]
    ppermute x6, waiting for transfers between devices: 14.8 us -> 28.1 us  [rep_sum(): lax.ppermute(part, 'rep', [(i, i ^ 1 << hop) for i in range(rep)])]
    squeeze x7 -> x0, local copies, waits for them, and re-layouts: 11.8 us -> none  [the longest x5 8.68 us: line_sum(): to_left = lax.dynamic_index_in_dim(blocks, at_left, 0, keepdims=False)]
  transfers between devices with their start and end apart: 61 -> 18, of which waited for: 11 -> 5; matrix products, arithmetic and copies ran while one was open for 6% -> 0% of each run, Pallas kernels for 17% -> 7%
where the time goes in v2:
time: 660 us; the launch traced here: 651 us
  Pallas kernels  582 us (88%)
  waiting for transfers between devices  28.2 us (4%)
  local copies, waits for them, and re-layouts  15.2 us (2%)
  blocking collectives  9.77 us (1%)
  other arithmetic  7.32 us (1%)
  starting transfers between devices  7.22 us (1%)
    pallas_call x1, Pallas kernels, backward(): pl.pallas_call(functools.partial(back_kernel, names=names, line=line), in...  317 us
    pallas_call x1, Pallas kernels, gather(): pl.pallas_call(functools.partial(gather_kernel, count=count, line=n // 2,...  147 us
    pallas_call x6, Pallas kernels, adam_piece(): pl.pallas_call(functools.partial(adam_kernel, terms=len(terms), rate=rate...  30.4 us
    pallas_call x1, Pallas kernels, ffn(): pl.pallas_call(ffn_kernel, grid_spec=pltpu.PrefetchScalarGridSpec(num_sca...  29 us
    ppermute x6, waiting for transfers between devices, rep_sum(): lax.ppermute(part, 'rep', [(i, i ^ 1 << hop) for i in range(rep)])  28.1 us
    pallas_call x6, Pallas kernels, outer_piece(): pl.pallas_call(functools.partial(outer_kernel, groups=groups), grid_spec=...  25.3 us
    pallas_call x1, Pallas kernels, attention(): pl.pallas_call(attn_kernel, grid_spec=pltpu.PrefetchScalarGridSpec(num_sc...  20.9 us
  transfers between devices with their start and end apart: 18, of which 5 were waited for; matrix products, arithmetic and copies ran while one was open for 0% of the time, Pallas kernels for 7%

profile of v2, /device:TPU:0, one launch (start us, length us, event | category | flops | bytes accessed | tf_op | source)
XLA Modules:
  0.0 651.4 jit_solution(12452444542107368817)
XLA Ops:
  0.7 2.2 convert_element_type.125
  2.9 1.1 slice.22.refs_3_
  4.0 0.9 slice.20.refs_1_
  4.9 0.1 convert_element_type.126
  5.1 1.0 slice_bitcast_fusion
  6.1 0.6 pad.4.refs_0_
  6.7 147.4 %gather.1 = (bf16[8,64,256]{2,1,0:T(8,128)(2,1)}, bf16[8,256,1536]{2,1,0:T(8,128)(2,1)}, bf16[8,128,2048]{2,1,0:T(8,128)(2,1)}, bf16[8,256,2048]{2,1,0:T(8,128)(2,1)}, bf16[8,128,2048]{2,1,0:T(8,128)(2,1)}) custom-call(bf16[64,256]{1,0:T(8,128)(2,1)} %pad.4.refs_0_, bf16[256,1536]{1,0:T(8,128)(2,1)} %slice.20.refs_1_, ...), custom_call_target="tpu_custom_call" | custom-call | bytes 209715200 | tf_op jit(solution)/shard_map/gather/pallas_call | solution.py:722
  154.2 1.4 slice_convert_fusion
  155.6 1.0 copy.69.ids_ref
  156.6 12.3 %norm_qkv.1 = (bf16[1024,2048]{1,0:T(8,128)(2,1)}, bf16[1024,1536]{1,0:T(8,128)(2,1)}) custom-call(bf16[1024,2048]{1,0:T(8,128)(2,1)} %bitcast.94, f32[8,2048]{1,0:T(8,128)} %bitcast.85, bf16[2048,1536]{1,0:T(8,128)(2,1)} %bitcast.92), custom_call_target="tpu_custom_call" | custom-call | flops 6442450944 | bytes 14680064 | tf_op jit(solution)/shard_map/norm_qkv/pallas_call | solution.py:46
  168.9 20.9 %attention.1 = (bf16[1024,1024]{1,0:T(8,128)(2,1)}, f32[16,1024]{1,0:T(8,128)}) custom-call(s32[4]{0:T(128)} %bitcast.103, bf16[1024,1536]{1,0:T(8,128)(2,1)} %get-tuple-element.109.q_ref.k_ref.v_ref.refs_11_, bf16[1024,1536]{1,0:T(8,128)(2,1)} %get-tuple-element.109.q_ref.k_ref.v_ref.refs_11_, bf16[1024,1536]{1,0:T(8,128)(2,1)} %get-tuple-element.109.q_ref.k_ref.v_ref.refs_11_), custom_call_target="tpu_custom_call" | custom-call | flops 17179869184 | bytes 16777216 | tf_op jit(solution)/shard_map/attention/pallas_call | solution.py:127
  189.8 0.7 pad_add_fusion.place_ref
  190.4 29.0 %ffn.1 = (f32[1024,2048]{1,0:T(8,128)}, bf16[1024,2048]{1,0:T(8,128)(2,1)}, bf16[1024,1024]{1,0:T(8,128)(2,1)}, bf16[1024,2048]{1,0:T(8,128)(2,1)}, bf16[1024,2048]{1,0:T(8,128)(2,1)}, /*index=5*/f32[1024,128]{1,0:T(8,128)}) custom-call(s32[8]{0:T(128)} %table_ref.1, bf16[1024,2048]{1,0:T(8,128)(2,1)} %bitcast.95, ...), custom_call_target="tpu_custom_call" | custom-call | flops 17179869184 | bytes 41943040 | tf_op jit(solution)/shard_map/ffn/pallas_call | solution.py:291
  219.4 316.9 %backward.1 = (bf16[1024,2048]{1,0:T(8,128)(2,1)}, f32[1024,2048]{1,0:T(8,128)}, bf16[1024,2048]{1,0:T(8,128)(2,1)}, bf16[1024,1024]{1,0:T(8,128)(2,1)}, bf16[10...) custom-call(s32[4]{0:T(128)} %bitcast.104, ...), custom_call_target="tpu_custom_call" | custom-call | flops 214748364800 | bytes 419430400 | tf_op jit(solution)/shard_map/backward/pallas_call | solution.py:1036
  536.3 5.8 adam.10
  542.1 5.8 adam.11
  547.9 0.6 collective-permute-start.12
  548.5 4.9 adam.6
  553.3 0.1 collective-permute-start.9
  553.4 4.9 adam.7
  558.3 0.5 collective-permute-start.6
  558.8 4.9 adam.8
  563.8 4.2 adam.9
  568.0 0.1 collective-permute-start
  568.2 9.8 %psum.7 = f32[2,256]{1,0:T(2,128)S(1)} all-reduce(f32[2,256]{1,0:T(2,128)S(1)} %subtract_subtract_fusion), channel_id=1, replica_groups=mesh['rep'=4,'fsdp'=8] {'rep'}, use_global_device_ids=true, to_apply=%region_2.3 | all-reduce | flops 512 | bytes 4096 | tf_op jit(solution)/shard_map/psum | solution.py:1153
  578.0 0.6 fusion.6
  578.6 0.1 collective-permute-start.3
  578.7 0.9 add_convert_fusion.11
  579.6 0.5 collective-permute-start.1
  580.1 0.1 add_convert_fusion.1
  580.2 1.7 collective-permute-start.16
  581.9 0.5 collective-permute-start.13
  582.4 0.1 add_convert_fusion.5
  582.5 1.7 collective-permute-start.10
  584.2 0.1 add_convert_fusion.7
  584.3 0.5 collective-permute-start.7
  584.7 0.1 add_convert_fusion.9
  584.8 6.8 %collective-permute-done.16 = bf16[64,2048]{1,0:T(8,128)(2,1)S(1)} collective-permute-done((bf16[64,2048]{1,0:T(8,128)(2,1)S(1)}, bf16[64,2048]{1,0:T(8,128)(2,1)S(1)}, u32[]{:S(2)}, u32[]{:S(2)}) %collective-permute-start.16) | collective-permute-done | bytes 262176 | tf_op jit(solution)/shard_map/ppermute | solution.py:580
  591.6 0.4 collective-permute-start.4
  592.0 0.1 add_convert_fusion.keep_ref
  592.1 5.1 collective-permute-done.13
  597.2 0.1 add_convert_fusion.2.keep_ref
  597.3 5.5 collective-permute-done.10
  602.8 0.1 add_convert_fusion.4.keep_ref
  602.9 5.5 collective-permute-done.7
  608.4 0.1 add_convert_fusion.6.keep_ref
  608.5 5.1 collective-permute-done.4
  613.7 0.1 add_convert_fusion.8.keep_ref
  613.8 0.6 collective-permute-start.5
  614.4 0.1 collective-permute-start.2
  614.5 0.6 fusion
  615.1 4.9 outer.10
  620.1 0.7 copy-done.17
  620.8 4.0 outer.6
  624.8 0.7 copy-done.15
  625.5 4.9 outer.11
  630.4 0.7 copy-done.9
  631.1 4.0 outer.7
  635.2 0.7 copy-done.8
  635.9 4.0 outer.8
  639.9 0.6 copy-done.18
  640.6 3.4 outer.9
  644.0 4.9 copy.100
  648.9 2.0 copy.101
  (75 shorter events, 0.4 us)
Async XLA Ops:
  2.9 2.0 copy-start
  4.9 1.2 copy-start.21
  5.1 150.5 %copy-start.25 = (s32[1,1024]{1,0:T(1,128)S(1)}, s32[1,1024]{1,0:T(1,128)}, u32[]{:S(2)}) copy-start(s32[1,1024]{1,0:T(1,128)} %param.20) | copy-start | bytes 12292
  542.1 37.5 %collective-permute-start.15 = (bf16[64,2048]{1,0:T(8,128)(2,1)}, bf16[64,2048]{1,0:T(8,128)(2,1)S(1)}, u32[]{:S(2)}, u32[]{:S(2)}) collective-permute-start(bf16[64,2048]{1,0:T(8,128)(2,1)} %get-tuple-element.179), channel_id=1, source_target_pairs={{0,8},{8,0},{16,24},{24,16},{1,9},{9,1},{17,25},{25,17},{2,10},{10... | collective-permute-start | bytes 786440 | tf_op jit(solution)/shard_map/ppermute | solution.py:578
  547.9 32.2 %collective-permute-start.12 = (bf16[64,2048]{1,0:T(8,128)(2,1)}, bf16[64,2048]{1,0:T(8,128)(2,1)S(1)}, u32[]{:S(2)}, u32[]{:S(2)}) collective-permute-start(bf16[64,2048]{1,0:T(8,128)(2,1)} %get-tuple-element.177), channel_id=1, source_target_pairs={{0,8},{8,0},{16,24},{24,16},{1,9},{9,1},{17,25},{25,17},{2,10},{10... | collective-permute-start | bytes 786440 | tf_op jit(solution)/shard_map/ppermute | solution.py:578
  553.3 28.6 %collective-permute-start.9 = (bf16[128,1024]{1,0:T(8,128)(2,1)}, bf16[128,1024]{1,0:T(8,128)(2,1)S(1)}, u32[]{:S(2)}, u32[]{:S(2)}) collective-permute-start(bf16[128,1024]{1,0:T(8,128)(2,1)} %get-tuple-element.162), channel_id=1, source_target_pairs={{0,8},{8,0},{16,24},{24,16},{1,9},{9,1},{17,25},{25,17},{2,10},{10... | collective-permute-start | bytes 786440 | tf_op jit(solution)/shard_map/ppermute | solution.py:578
  558.3 24.2 %collective-permute-start.6 = (bf16[128,1024]{1,0:T(8,128)(2,1)}, bf16[128,1024]{1,0:T(8,128)(2,1)S(1)}, u32[]{:S(2)}, u32[]{:S(2)}) collective-permute-start(bf16[128,1024]{1,0:T(8,128)(2,1)} %get-tuple-element.160), channel_id=1, source_target_pairs={{0,8},{8,0},{16,24},{24,16},{1,9},{9,1},{17,25},{25,17},{2,10},{10... | collective-permute-start | bytes 786440 | tf_op jit(solution)/shard_map/ppermute | solution.py:578
  563.7 4.4 copy-start.19
  563.7 4.4 copy-start.22
  563.7 4.4 copy-start.23
  563.7 4.4 copy-start.24
  563.7 14.3 %copy-start.26 = (f32[2,256]{1,0:T(2,128)S(1)}, f32[2,256]{1,0:T(2,128)}, u32[]{:S(2)}) copy-start(f32[2,256]{1,0:T(2,128)} %param.33) | copy-start | bytes 6148
  563.7 14.8 %copy-start.27 = (bf16[128,1024]{1,0:T(8,128)(2,1)S(1)}, bf16[128,1024]{1,0:T(8,128)(2,1)}, u32[]{:S(2)}) copy-start(bf16[128,1024]{1,0:T(8,128)(2,1)} %get-tuple-element.158) | copy-start | bytes 786436
  563.8 16.3 %copy-start.11 = (bf16[64,2048]{1,0:T(8,128)(2,1)S(1)}, bf16[64,2048]{1,0:T(8,128)(2,1)}, u32[]{:S(2)}) copy-start(bf16[64,2048]{1,0:T(8,128)(2,1)} %get-tuple-element.178) | copy-start | bytes 786436
  563.8 18.1 %copy-start.10 = (bf16[64,2048]{1,0:T(8,128)(2,1)S(1)}, bf16[64,2048]{1,0:T(8,128)(2,1)}, u32[]{:S(2)}) copy-start(bf16[64,2048]{1,0:T(8,128)(2,1)} %get-tuple-element.176) | copy-start | bytes 786436
  563.8 18.6 %copy-start.12 = (bf16[128,1024]{1,0:T(8,128)(2,1)S(1)}, bf16[128,1024]{1,0:T(8,128)(2,1)}, u32[]{:S(2)}) copy-start(bf16[128,1024]{1,0:T(8,128)(2,1)} %get-tuple-element.161) | copy-start | bytes 786436
  568.0 16.2 %copy-start.13 = (bf16[128,1024]{1,0:T(8,128)(2,1)S(1)}, bf16[128,1024]{1,0:T(8,128)(2,1)}, u32[]{:S(2)}) copy-start(bf16[128,1024]{1,0:T(8,128)(2,1)} %get-tuple-element.159) | copy-start | bytes 786436
  568.0 16.7 %copy-start.14 = (bf16[128,1024]{1,0:T(8,128)(2,1)S(1)}, bf16[128,1024]{1,0:T(8,128)(2,1)}, u32[]{:S(2)}) copy-start(bf16[128,1024]{1,0:T(8,128)(2,1)} %get-tuple-element.157) | copy-start | bytes 786436
  568.0 10.6 %collective-permute-start = (bf16[128,512]{1,0:T(8,128)(2,1)}, bf16[128,512]{1,0:T(8,128)(2,1)S(1)}, u32[]{:S(2)}, u32[]{:S(2)}) collective-permute-start(bf16[128,512]{1,0:T(8,128)(2,1)} %get-tuple-element.156), channel_id=1, source_target_pairs={{0,8},{8,0},{16,24},{24,16},{1,9},{9,1},{17,25},{25,17},{2,10},{10... | collective-permute-start | bytes 393224 | tf_op jit(solution)/shard_map/ppermute | solution.py:578
  568.2 46.3 %copy-start.20 = (f32[2,256]{1,0:T(2,128)}, f32[2,256]{1,0:T(2,128)S(1)}, u32[]{:S(2)}) copy-start(f32[2,256]{1,0:T(2,128)S(1)} %bitcast_reduce_fusion) | copy-start | bytes 6148
  578.6 5.7 collective-permute-start.3
  579.6 34.1 %collective-permute-start.1 = (bf16[128,512]{1,0:T(8,128)(2,1)S(1)}, bf16[128,512]{1,0:T(8,128)(2,1)S(1)}, u32[]{:S(2)}, u32[]{:S(2)}) collective-permute-start(bf16[128,512]{1,0:T(8,128)(2,1)S(1)} %add_convert_fusion.11), channel_id=1, source_target_pairs={{0,16},{8,24},{16,0},{24,8},{1,17},{9,25},{17,1},{25,9},{2,18},{10... | collective-permute-start | bytes 393224 | tf_op jit(solution)/shard_map/ppermute | solution.py:580
  580.2 11.4 %collective-permute-start.16 = (bf16[64,2048]{1,0:T(8,128)(2,1)S(1)}, bf16[64,2048]{1,0:T(8,128)(2,1)S(1)}, u32[]{:S(2)}, u32[]{:S(2)}) collective-permute-start(bf16[64,2048]{1,0:T(8,128)(2,1)S(1)} %add_convert_fusion.1), channel_id=1, source_target_pairs={{0,16},{8,24},{16,0},{24,8},{1,17},{9,25},{17,1},{25,9},{2,18},{10... | collective-permute-start | bytes 786440 | tf_op jit(solution)/shard_map/ppermute | solution.py:580
  581.9 15.3 %collective-permute-start.13 = (bf16[64,2048]{1,0:T(8,128)(2,1)S(1)}, bf16[64,2048]{1,0:T(8,128)(2,1)S(1)}, u32[]{:S(2)}, u32[]{:S(2)}) collective-permute-start(bf16[64,2048]{1,0:T(8,128)(2,1)S(1)} %add_convert_fusion.3), channel_id=1, source_target_pairs={{0,16},{8,24},{16,0},{24,8},{1,17},{9,25},{17,1},{25,9},{2,18},{10... | collective-permute-start | bytes 786440 | tf_op jit(solution)/shard_map/ppermute | solution.py:580
  582.5 20.3 %collective-permute-start.10 = (bf16[128,1024]{1,0:T(8,128)(2,1)S(1)}, bf16[128,1024]{1,0:T(8,128)(2,1)S(1)}, u32[]{:S(2)}, u32[]{:S(2)}) collective-permute-start(bf16[128,1024]{1,0:T(8,128)(2,1)S(1)} %add_convert_fusion.5), channel_id=1, source_target_pairs={{0,16},{8,24},{16,0},{24,8},{1,17},{9,25},{17,1},{25,9},{2,18},{10... | collective-permute-start | bytes 786440 | tf_op jit(solution)/shard_map/ppermute | solution.py:580
  584.3 24.2 %collective-permute-start.7 = (bf16[128,1024]{1,0:T(8,128)(2,1)S(1)}, bf16[128,1024]{1,0:T(8,128)(2,1)S(1)}, u32[]{:S(2)}, u32[]{:S(2)}) collective-permute-start(bf16[128,1024]{1,0:T(8,128)(2,1)S(1)} %add_convert_fusion.7), channel_id=1, source_target_pairs={{0,16},{8,24},{16,0},{24,8},{1,17},{9,25},{17,1},{25,9},{2,18},{10... | collective-permute-start | bytes 786440 | tf_op jit(solution)/shard_map/ppermute | solution.py:580
  591.6 22.1 %collective-permute-start.4 = (bf16[128,1024]{1,0:T(8,128)(2,1)S(1)}, bf16[128,1024]{1,0:T(8,128)(2,1)S(1)}, u32[]{:S(2)}, u32[]{:S(2)}) collective-permute-start(bf16[128,1024]{1,0:T(8,128)(2,1)S(1)} %add_convert_fusion.9), channel_id=1, source_target_pairs={{0,16},{8,24},{16,0},{24,8},{1,17},{9,25},{17,1},{25,9},{2,18},{10... | collective-permute-start | bytes 786440 | tf_op jit(solution)/shard_map/ppermute | solution.py:580
  592.1 23.1 %copy-start.5 = (bf16[64,2048]{1,0:T(8,128)(2,1)}, bf16[64,2048]{1,0:T(8,128)(2,1)S(1)}, u32[]{:S(2)}) copy-start(bf16[64,2048]{1,0:T(8,128)(2,1)S(1)} %add_convert_fusion.keep_ref) | copy-start | bytes 786436
  597.2 17.2 %collective-permute-start.17 = (bf16[64,2048]{1,0:T(8,128)(2,1)S(1)}, bf16[64,2048]{1,0:T(8,128)(2,1)S(1)}, u32[]{:S(2)}, u32[]{:S(2)}) collective-permute-start(bf16[64,2048]{1,0:T(8,128)(2,1)S(1)} %add_convert_fusion.keep_ref), channel_id=1, source_target_pairs={{0,8},{8,0},{16,24},{24,16},{1,9},{9,1},{17,25},{25,17},{2,10},{10... | collective-permute-start | bytes 786440 | tf_op jit(solution)/shard_map/ppermute | solution.py:581
  597.3 22.7 %copy-start.4 = (bf16[64,2048]{1,0:T(8,128)(2,1)}, bf16[64,2048]{1,0:T(8,128)(2,1)S(1)}, u32[]{:S(2)}) copy-start(bf16[64,2048]{1,0:T(8,128)(2,1)S(1)} %add_convert_fusion.2.keep_ref) | copy-start | bytes 786436
  602.8 22.0 %collective-permute-start.14 = (bf16[64,2048]{1,0:T(8,128)(2,1)S(1)}, bf16[64,2048]{1,0:T(8,128)(2,1)S(1)}, u32[]{:S(2)}, u32[]{:S(2)}) collective-permute-start(bf16[64,2048]{1,0:T(8,128)(2,1)S(1)} %add_convert_fusion.2.keep_ref), channel_id=1, source_target_pairs={{0,8},{8,0},{16,24},{24,16},{1,9},{9,1},{17,25},{25,17},{2,10},{10... | collective-permute-start | bytes 786440 | tf_op jit(solution)/shard_map/ppermute | solution.py:581
  602.9 17.1 %copy-start.6 = (bf16[128,1024]{1,0:T(8,128)(2,1)}, bf16[128,1024]{1,0:T(8,128)(2,1)S(1)}, u32[]{:S(2)}) copy-start(bf16[128,1024]{1,0:T(8,128)(2,1)S(1)} %add_convert_fusion.4.keep_ref) | copy-start | bytes 786436
  608.4 11.6 %collective-permute-start.11 = (bf16[128,1024]{1,0:T(8,128)(2,1)S(1)}, bf16[128,1024]{1,0:T(8,128)(2,1)S(1)}, u32[]{:S(2)}, u32[]{:S(2)}) collective-permute-start(bf16[128,1024]{1,0:T(8,128)(2,1)S(1)} %add_convert_fusion.4.keep_ref), channel_id=1, source_target_pairs={{0,8},{8,0},{16,24},{24,16},{1,9},{9,1},{17,25},{25,17},{2,10},{10... | collective-permute-start | bytes 786440 | tf_op jit(solution)/shard_map/ppermute | solution.py:581
  608.5 11.5 %copy-start.3 = (bf16[128,1024]{1,0:T(8,128)(2,1)}, bf16[128,1024]{1,0:T(8,128)(2,1)S(1)}, u32[]{:S(2)}) copy-start(bf16[128,1024]{1,0:T(8,128)(2,1)S(1)} %add_convert_fusion.6.keep_ref) | copy-start | bytes 786436
  613.7 16.8 %collective-permute-start.8 = (bf16[128,1024]{1,0:T(8,128)(2,1)S(1)}, bf16[128,1024]{1,0:T(8,128)(2,1)S(1)}, u32[]{:S(2)}, u32[]{:S(2)}) collective-permute-start(bf16[128,1024]{1,0:T(8,128)(2,1)S(1)} %add_convert_fusion.6.keep_ref), channel_id=1, source_target_pairs={{0,8},{8,0},{16,24},{24,16},{1,9},{9,1},{17,25},{25,17},{2,10},{10... | collective-permute-start | bytes 786440 | tf_op jit(solution)/shard_map/ppermute | solution.py:581
  613.7 11.1 %copy-start.2 = (bf16[128,1024]{1,0:T(8,128)(2,1)}, bf16[128,1024]{1,0:T(8,128)(2,1)S(1)}, u32[]{:S(2)}) copy-start(bf16[128,1024]{1,0:T(8,128)(2,1)S(1)} %add_convert_fusion.8.keep_ref) | copy-start | bytes 786436
  613.8 21.4 %collective-permute-start.5 = (bf16[128,1024]{1,0:T(8,128)(2,1)S(1)}, bf16[128,1024]{1,0:T(8,128)(2,1)S(1)}, u32[]{:S(2)}, u32[]{:S(2)}) collective-permute-start(bf16[128,1024]{1,0:T(8,128)(2,1)S(1)} %add_convert_fusion.8.keep_ref), channel_id=1, source_target_pairs={{0,8},{8,0},{16,24},{24,16},{1,9},{9,1},{17,25},{25,17},{2,10},{10... | collective-permute-start | bytes 786440 | tf_op jit(solution)/shard_map/ppermute | solution.py:581
  614.4 10.4 %copy-start.7 = (bf16[128,512]{1,0:T(8,128)(2,1)}, bf16[128,512]{1,0:T(8,128)(2,1)S(1)}, u32[]{:S(2)}) copy-start(bf16[128,512]{1,0:T(8,128)(2,1)S(1)} %add_convert_fusion.10.keep_ref) | copy-start | bytes 393220
  614.4 0.7 copy-start.16
  614.4 25.5 %collective-permute-start.2 = (bf16[128,512]{1,0:T(8,128)(2,1)S(1)}, bf16[128,512]{1,0:T(8,128)(2,1)S(1)}, u32[]{:S(2)}, u32[]{:S(2)}) collective-permute-start(bf16[128,512]{1,0:T(8,128)(2,1)S(1)} %add_convert_fusion.10.keep_ref), channel_id=1, source_target_pairs={{0,8},{8,0},{16,24},{24,16},{1,9},{9,1},{17,25},{25,17},{2,10},{10... | collective-permute-start | bytes 393224 | tf_op jit(solution)/shard_map/ppermute | solution.py:581
  620.1 0.7 copy-start.17
  624.8 0.7 copy-start.15
  630.4 0.7 copy-start.9
  635.2 0.7 copy-start.8
  639.9 0.7 copy-start.18
  644.0 4.9 copy-start.1
